TPU v7x, 256 devices: a whole 4x4x8 slice. The times are simulated.
256 devices in a mesh: frame: 32 (over x, z_lo, core), patch: 8 (over z_hi, y).
Axes of the slice: x: 4, y: 4, z: 8 (z_hi: 2, z_lo: 4; z = z_hi * 4 + z_lo), core: 2. Of those that a mesh axis runs over, the one named last changes fastest.
Arguments:
- clip: bfloat16 [4, 32, 1024, 1280], P(None, 'frame', 'patch'), may hold values from -54 to 54
- norm_time: float32 [1280], replicated, may hold values from 0.1 to 1.9
- w_time_qkv: bfloat16 [1280, 1920], replicated, may hold values from -0.15625 to 0.15625
- q_gain_time: float32 [640], replicated, may hold values from 1 to 2
- k_gain_time: float32 [640], replicated, may hold values from 1 to 2
- w_time_out: bfloat16 [640, 1280], replicated, may hold values from -0.25 to 0.25
- norm_space: float32 [1280], replicated, may hold values from 0.1 to 1.9
- w_space_qkv: bfloat16 [1280, 1920], replicated, may hold values from -0.15625 to 0.15625
- q_gain_space: float32 [640], replicated, may hold values from 1 to 2
- k_gain_space: float32 [640], replicated, may hold values from 1 to 2
Outputs:
- spatial_out: bfloat16 [4, 32, 1024, 640], P(None, 'frame', 'patch')
All inputs are finite; a program needn't handle non-finite values.
Results may differ from a plain program's by a relative error of at most 0.025.
Values may be sent and summed in bfloat16 or wider, within the bound.
A program may use at most 128 MiB of HBM per device.

v0:
```python
import jax
import jax.numpy as jnp
from jax import lax
from jax.sharding import PartitionSpec as P

HDIM = 80


epsilon = 1e-06


def layer_norm(token_rows, norm_gain):
    values = token_rows.astype(jnp.float32)
    average = jnp.mean(values, axis=-1, keepdims=True)
    centred = values - average
    variance = jnp.mean(centred * centred, axis=-1, keepdims=True)
    return (centred * lax.rsqrt(variance + epsilon) * norm_gain).astype(jnp.bfloat16)


def head_norm(projected, head_gain, head_size):
    leading = projected.shape[:-1]
    split_heads = projected.reshape(leading + (projected.shape[-1] // head_size, head_size))
    squares = jnp.mean(split_heads * split_heads, axis=-1, keepdims=True)
    scaled = split_heads * lax.rsqrt(squares + epsilon)
    return (scaled.reshape(projected.shape) * head_gain).astype(jnp.bfloat16)


def project_heads(normed, weight, query_gain, key_gain, head_size):
    inner_width = weight.shape[1] // 3
    product = jnp.dot(normed, weight, preferred_element_type=jnp.float32)
    query = head_norm(product[:, :inner_width], query_gain, head_size)
    keys = head_norm(product[:, inner_width : 2 * inner_width], key_gain, head_size)
    values = product[:, 2 * inner_width :].astype(jnp.bfloat16)
    return (query, keys, values)


def frame_attention(query, keys, values):
    clip_count, frame_count, patch_count, inner_width = query.shape
    split = (clip_count, frame_count, patch_count, inner_width // HDIM, HDIM)
    scores = jnp.einsum(
        "cfphd,cgphd->cphfg",
        query.reshape(split),
        keys.reshape(split),
        preferred_element_type=jnp.float32,
    ) * HDIM ** (-0.5)
    exponent = jnp.exp(scores)
    totals = jnp.sum(exponent, axis=-1)
    summed = jnp.einsum(
        "cphfg,cgphd->cfphd",
        exponent.astype(jnp.bfloat16),
        values.reshape(split),
        preferred_element_type=jnp.float32,
    )
    result = summed / jnp.transpose(totals, (0, 3, 1, 2))[..., None]
    result = result.reshape(query.shape).astype(jnp.bfloat16)
    return lax.all_to_all(result, "frame", split_axis=1, concat_axis=2, tiled=True)


def space_start(query):
    clip_count = query.shape[0]
    row_count = query.shape[2]
    head_count = query.shape[3] // HDIM
    query_heads = query.reshape(clip_count, row_count, head_count, HDIM)
    empty = (
        jnp.zeros((clip_count, head_count, row_count), jnp.float32),
        jnp.zeros((clip_count, row_count, head_count, HDIM), jnp.float32),
    )
    return (query_heads, empty)


def space_add(query_heads, keys, values):
    split = (keys.shape[0], keys.shape[2], query_heads.shape[2], HDIM)
    scores = jnp.einsum(
        "cqhd,ckhd->chqk", query_heads, keys.reshape(split), preferred_element_type=jnp.float32
    ) * HDIM ** (-0.5)
    exponent = jnp.exp(scores)
    totals = jnp.sum(exponent, axis=-1)
    summed = jnp.einsum(
        "chqk,ckhd->cqhd",
        exponent.astype(jnp.bfloat16),
        values.reshape(split),
        preferred_element_type=jnp.float32,
    )
    return (totals, summed)


def space_finish(totals, summed):
    result = summed / jnp.transpose(totals, (0, 2, 1))[..., None]
    return result.reshape(
        summed.shape[0], 1, summed.shape[1], summed.shape[2] * summed.shape[3]
    ).astype(jnp.bfloat16)


def body(
    clip,
    norm_time,
    w_time_qkv,
    q_gain_time,
    k_gain_time,
    w_time_out,
    norm_space,
    w_space_qkv,
    q_gain_space,
    k_gain_space,
):
    clip_count, frame_count, pat_count, features = clip.shape
    inner_width = w_time_out.shape[0]
    token_rows = clip.reshape(-1, features)
    normed = layer_norm(token_rows, norm_time)
    local_shape = (clip_count, frame_count, pat_count, inner_width)
    query, keys, values = project_heads(normed, w_time_qkv, q_gain_time, k_gain_time, HDIM)
    pieces = (
        lax.all_to_all(
            query.reshape(local_shape), "frame", split_axis=2, concat_axis=1, tiled=True
        ),
        lax.all_to_all(keys.reshape(local_shape), "frame", split_axis=2, concat_axis=1, tiled=True),
        lax.all_to_all(
            values.reshape(local_shape), "frame", split_axis=2, concat_axis=1, tiled=True
        ),
    )
    attended = frame_attention(pieces[0], pieces[1], pieces[2])
    delta = jnp.dot(
        attended.reshape(-1, inner_width), w_time_out, preferred_element_type=jnp.float32
    )
    mixed = (token_rows.astype(jnp.float32) + delta).astype(jnp.bfloat16)
    space_normed = layer_norm(mixed, norm_space)
    space_query, space_keys, space_values = project_heads(
        space_normed, w_space_qkv, q_gain_space, k_gain_space, HDIM
    )
    space_query = space_query.reshape(local_shape)
    space_keys = space_keys.reshape(local_shape)
    space_values = space_values.reshape(local_shape)
    query_heads, empty = space_start(space_query)
    pieces = (
        lax.all_gather(space_keys, "patch", axis=2, tiled=True),
        lax.all_gather(space_values, "patch", axis=2, tiled=True),
    )
    totals, summed = space_add(query_heads, pieces[0], pieces[1])
    spatial = space_finish(totals, summed)
    return spatial


def solution(mesh):
    in_specs = (P(None, "frame", "patch", None), P(), P(), P(), P(), P(), P(), P(), P(), P())
    out_specs = P(None, "frame", "patch", None)
    return jax.shard_map(body, mesh=mesh, in_specs=in_specs, out_specs=out_specs, check_vma=False)
```

profile of v0, /device:TPU:1, one launch (start us, length us, event | category | flops | bytes accessed | tf_op | source)
XLA Modules:
  0.0 441.8 jit_solution(10518621939895645860)
XLA Ops:
  9.3 4.9 %fusion.38 = f32[512,1920]{1,0:T(8,128)S(1)} fusion(bf16[512,1280]{1,0:T(8,128)(2,1)S(1)} %fusion.13, bf16[1280,1920]{1,0:T(8,128)(2,1)} %param.12), kind=kOutput, calls=%fused_computation.59 | convolution fusion | flops 2516582400 | bytes 10158080 | tf_op jit(solution)/shard_map/dot_general | solution.py:30
  14.3 1.8 slice_multiply_fusion.3
  17.0 2.8 copy.55
  22.4 2.8 copy.56
  25.3 2.8 copy.59
  30.8 2.8 copy.60
  33.6 3.6 multiply_convert_fusion.3
  38.5 10.1 %all-to-all-start.1 = ((bf16[4,1,128,640]{3,0,1,2:T(4,128)(2,1)}), bf16[4,1,128,640]{3,0,1,2:T(4,128)(2,1)}, u32[]{:S(2)}, u32[]{:S(2)}) async-start(bf16[4,1,128,640]{3,0,1,2:T(4,128)(2,1)} %copy.57), calls=%async_computation.1 | async-start | bytes 1310720 | tf_op jit(solution)/shard_map/all_to_all | solution.py:113
  48.6 2.4 copy.61
  51.0 17.2 %all-to-all-done.1 = bf16[4,1,128,640]{3,0,1,2:T(4,128)(2,1)} async-done(((bf16[4,1,128,640]{3,0,1,2:T(4,128)(2,1)}), bf16[4,1,128,640]{3,0,1,2:T(4,128)(2,1)}, u32[]{:S(2)}, u32[]{:S(2)}) %all-to-all-start.1) | async-done | bytes 655392 | tf_op jit(solution)/shard_map/all_to_all | solution.py:113
  68.2 4.4 all-to-all-start.2
  75.4 17.0 %all-to-all-done.2 = bf16[4,1,128,640]{3,0,1,2:T(4,128)(2,1)} async-done(((bf16[4,1,128,640]{3,0,1,2:T(4,128)(2,1)}), bf16[4,1,128,640]{3,0,1,2:T(4,128)(2,1)}, u32[]{:S(2)}, u32[]{:S(2)}) %all-to-all-start.2) | async-done | bytes 655392 | tf_op jit(solution)/shard_map/all_to_all | solution.py:116
  92.4 4.4 all-to-all-start
  97.0 3.0 reshape.187
  100.1 3.0 reshape.188
  103.0 4.6 %fusion.15 = (f32[4,4,8,32]{3,2,1,0:T(8,128)S(1)}, f32[4,4,8,32,32]{3,4,2,1,0:T(8,128)}) fusion(bf16[4,32,4,8,80]{4,3,0,2,1:T(8,128)(2,1)} %reshape.188, bf16[4,32,4,8,80]{4,3,0,2,1:T(8,128)(2,1)} %reshape.187), kind=kOutput, calls=%fused_computation.23 | convolution fusion | flops 21229568 | bytes 1851392 | tf_op jit(solution)/shard_map/cfphd,cgphd->cphfg/dot_general | solution.py:40
  107.7 8.9 %all-to-all-done = bf16[4,1,128,640]{3,0,1,2:T(4,128)(2,1)} async-done(((bf16[4,1,128,640]{3,0,1,2:T(4,128)(2,1)}), bf16[4,1,128,640]{3,0,1,2:T(4,128)(2,1)}, u32[]{:S(2)}, u32[]{:S(2)}) %all-to-all-start) | async-done | bytes 655392 | tf_op jit(solution)/shard_map/all_to_all | solution.py:117
  116.5 3.0 reshape.186
  119.5 3.4 fusion.14
  124.4 3.1 reshape.189
  127.5 23.4 %all_to_all.16 = bf16[4,32,4,640]{3,2,0,1:T(4,128)(2,1)S(1)} all-to-all(bf16[4,32,4,640]{3,2,0,1:T(4,128)(2,1)} %reshape.189), channel_id=1, replica_groups=mesh['frame'=32,'patch'=8] {'frame'}, dimensions={1} | all-to-all | bytes 1310720 | tf_op jit(solution)/shard_map/all_to_all | solution.py:56
  152.0 2.2 reshape.180
  154.2 2.4 convert_reduce_fusion
  157.1 5.1 %fusion.20 = f32[512,1920]{1,0:T(8,128)S(1)} fusion(bf16[1280,1920]{1,0:T(8,128)(2,1)} %param.17, bf16[512,1280]{1,0:T(8,128)(2,1)S(1)} %get-tuple-element.18, f32[1280]{0:T(1024)S(1)} %copy-done.12, f32[512]{0:T(512)S(1)} %add_rsqrt_fusion.4, f32[512]{0:T(512)S(1)} %broadcast_multiply_fusion), kind=kOutput, calls=%fused_computation.26 | convolution fusion | flops 2519859200 | bytes 10167296 | tf_op jit(solution)/shard_map/dot_general | solution.py:30
  170.9 3.4 multiply_convert_fusion.1
  174.7 2.2 slice.42
  178.0 117.3 %all-gather.5.cloned.1.call-done = bf16[4,1,1024,640]{3,2,0,1:T(8,128)(2,1)} async-done(((bf16[4,1,128,640]{3,2,0,1:T(8,128)(2,1)}), bf16[4,1,1024,640]{3,2,0,1:T(8,128)(2,1)}) %all-gather.5.cloned.1.call-update) | async-done | bytes 5242896 | tf_op jit(solution)/shard_map/all_gather | solution.py:135
  295.3 8.0 %copy.76 = bf16[4,1,1024,640]{2,3,0,1:T(8,128)(2,1)} copy(bf16[4,1,1024,640]{3,2,0,1:T(8,128)(2,1)} %all-gather.5.cloned.1.call-done) | data formatting | bytes 10485760 | tf_op jit(solution)/shard_map/all_gather | solution.py:135
  303.3 11.8 %fusion = (f32[4,8,128]{2,1,0:T(8,128)S(1)}, f32[4,8,128,1024]{3,2,1,0:T(8,128)}) fusion(bf16[4,1024,8,80]{1,3,2,0:T(8,128)(2,1)} %bitcast.56, bf16[4,128,8,80]{3,2,1,0:T(8,128)(2,1)S(1)} %reshape.190), kind=kOutput, calls=%fused_computation.1 | convolution fusion | flops 679473152 | bytes 22691840 | tf_op jit(solution)/shard_map/cqhd,ckhd->chqk/dot_general | solution.py:73
  315.1 100.4 %all-gather.3.cloned.1.call-done = bf16[4,1,1024,640]{3,2,0,1:T(8,128)(2,1)} async-done(((bf16[4,1,128,640]{3,2,0,1:T(8,128)(2,1)}), bf16[4,1,1024,640]{3,2,0,1:T(8,128)(2,1)}) %all-gather.3.cloned.1.call-update) | async-done | bytes 5242896 | tf_op jit(solution)/shard_map/all_gather | solution.py:136
  415.5 8.0 %copy.70 = bf16[4,1,1024,640]{2,3,0,1:T(8,128)(2,1)} copy(bf16[4,1,1024,640]{3,2,0,1:T(8,128)(2,1)} %all-gather.3.cloned.1.call-done) | data formatting | bytes 10485760 | tf_op jit(solution)/shard_map/all_gather | solution.py:136
  423.5 10.4 %divide_convert_fusion = bf16[4,128,8,80]{1,3,2,0:T(8,128)(2,1)S(1)} fusion(bf16[4,1024,8,80]{1,3,2,0:T(8,128)(2,1)} %bitcast.57, f32[4,8,128,1024]{3,2,1,0:T(8,128)} %get-tuple-element.20, f32[4,128,8]{1,2,0:T(8,128)S(1)} %bitcast.74), kind=kOutput, calls=%fused_computation.29 | convolution fusion | flops 680132608 | bytes 22691840 | tf_op jit(solution)/shard_map/chqk,ckhd->cqhd/dot_general | solution.py:78
  (62 shorter events, 27.4 us)
Async XLA Ops:
  6.5 147.6 %copy-start = (bf16[640,1280]{1,0:T(8,128)(2,1)S(1)}, bf16[640,1280]{1,0:T(8,128)(2,1)}, u32[]{:S(2)}) copy-start(bf16[640,1280]{1,0:T(8,128)(2,1)} %param.15) | copy-start | bytes 4915204
  6.5 1.8 copy-start.2
  6.5 2.3 copy-start.7
  14.3 2.7 copy-start.3
  29.5 4.0 copy-start.8
  29.5 4.0 copy-start.9
  38.5 29.7 %all-to-all-start.1 = ((bf16[4,1,128,640]{3,0,1,2:T(4,128)(2,1)}), bf16[4,1,128,640]{3,0,1,2:T(4,128)(2,1)}, u32[]{:S(2)}, u32[]{:S(2)}) async-start(bf16[4,1,128,640]{3,0,1,2:T(4,128)(2,1)} %copy.57), calls=%async_computation.1 | async-start | bytes 1310720 | tf_op jit(solution)/shard_map/all_to_all | solution.py:113
  68.2 24.1 %all-to-all-start.2 = ((bf16[4,1,128,640]{3,0,1,2:T(4,128)(2,1)}), bf16[4,1,128,640]{3,0,1,2:T(4,128)(2,1)}, u32[]{:S(2)}, u32[]{:S(2)}) async-start(bf16[4,1,128,640]{3,0,1,2:T(4,128)(2,1)} %copy.61), calls=%async_computation.2 | async-start | bytes 1310720 | tf_op jit(solution)/shard_map/all_to_all | solution.py:116
  92.4 24.1 %all-to-all-start = ((bf16[4,1,128,640]{3,0,1,2:T(4,128)(2,1)}), bf16[4,1,128,640]{3,0,1,2:T(4,128)(2,1)}, u32[]{:S(2)}, u32[]{:S(2)}) async-start(bf16[4,1,128,640]{3,0,1,2:T(4,128)(2,1)} %copy.53), calls=%async_computation | async-start | bytes 1310720 | tf_op jit(solution)/shard_map/all_to_all | solution.py:117
  96.8 198.5 %all-gather.5.cloned.1.call-start = ((), (), s32[]{:S(2)}) async-start(), calls=%async_computation.5 | async-start | bytes 5898240 | tf_op jit(solution)/shard_map/all_gather | solution.py:135
  154.2 2.9 copy-start.12
  162.1 1.9 copy-start.4
  169.2 1.7 copy-start.5
  169.2 1.7 copy-start.10
  169.2 1.7 copy-start.11
  174.3 2.6 copy-start.6
  174.4 241.1 %all-gather.3.cloned.1.call-start = ((), (), s32[]{:S(2)}) async-start(), calls=%async_computation.4 | async-start | bytes 5898240 | tf_op jit(solution)/shard_map/all_gather | solution.py:136
  423.5 11.5 %copy-start.1 = (bf16[640,1280]{1,0:T(8,128)(2,1)S(1)}, bf16[640,1280]{1,0:T(8,128)(2,1)}, u32[]{:S(2)}) copy-start(bf16[640,1280]{1,0:T(8,128)(2,1)} %param.15) | copy-start | bytes 4915204
Sparse Core Ops, SparseCore 0:
  174.5 120.7 all-gather.4
  297.8 117.6 all-gather.2
where the time goes:
time: 443 us; the launch traced here: 442 us
  waiting for transfers between devices  261 us (59%)
  local copies, waits for them, and re-layouts  65.1 us (15%)
  matrix products  42.7 us (10%)
  blocking collectives  23.4 us (5%)
  starting transfers between devices  19.4 us (4%)
  other arithmetic  16.8 us (4%)
  between operations  13.7 us (3%)
    all_gather x1, waiting for transfers between devices, body(): lax.all_gather(space_keys, 'patch', axis=2, tiled=True)  117 us
    all_gather x1, waiting for transfers between devices, body(): lax.all_gather(space_values, 'patch', axis=2, tiled=True)  100 us
    all_to_all x1, blocking collectives, frame_attention(): lax.all_to_all(result, 'frame', split_axis=1, concat_axis=2, tiled=True)  23.4 us
    all_to_all x1, waiting for transfers between devices, body(): lax.all_to_all(query.reshape(local_shape), 'frame', split_axis=2, concat_...  17.2 us
    all_to_all x1, waiting for transfers between devices, body(): lax.all_to_all(keys.reshape(local_shape), 'frame', split_axis=2, concat_a...  17 us
    dot_general x1, matrix products, space_add(): jnp.einsum('cqhd,ckhd->chqk', query_heads, keys.reshape(split), preferred...  11.8 us
    mul x8, local copies, waits for them, and re-layouts, head_norm(): scaled = split_heads * lax.rsqrt(squares + epsilon)  11.3 us
    dot_general x1, matrix products, space_add(): jnp.einsum('chqk,ckhd->cqhd', exponent.astype(jnp.bfloat16), values.resha...  10.4 us
  transfers between devices with their start and end apart: 5, of which 5 were waited for; matrix products, arithmetic and copies ran while one was open for 9% of the time, Pallas kernels for 0%

commit v1 on v0

v1 whole, which is shorter than its diff:
```python
import math

import jax
import jax.numpy as jnp
from jax import lax
from jax.experimental import pallas as pl
from jax.experimental.pallas import tpu as pltpu
from jax.sharding import PartitionSpec as P

MESH = pl.DeviceIdType.MESH
HDIM = 80
HEADS = 8
D = 1280
INNER = 640
HALF = 384
EPS = 1e-06
SCALE = HDIM ** (-0.5) * math.log2(math.e)
BF = jnp.bfloat16
F32 = jnp.float32
WINDOWS = (0, 0, 128, 128, 256, 256, 384, 384)


def div(a, b):
    return lax.div(a, jnp.int32(b))


def rem(a, b):
    return lax.rem(a, jnp.int32(b))


def kernel(
    clip, norm_t, w_tqkv, qg_t, kg_t, w_out, norm_s, w_sqkv, qg_s, kg_s,
    out,
    wt, wo, ws, blocks, pmask, tok, tq, tk, tv, mixed, tok2, send_qkv, qkv, vm, att, home,
    wsem, s1, r1, s2, r2, sq, rq, s4, r4,
):
    frame, patch = lax.axis_index("frame"), lax.axis_index("patch")
    x, zl, core = div(frame, 8), rem(div(frame, 2), 4), rem(frame, 2)
    zh, y = div(patch, 4), rem(patch, 4)
    z = zh * 4 + zl
    c, zb = div(z, 2), rem(z, 2)

    def flip(zz, cc):
        return rem(zz + 1 + rem(div(cc + 1, 2), 2), 2)

    zh_src = flip(zb, c)
    pg_src = zh_src * 4 + y

    def is_me(device):
        return (device[0] == frame) & (device[1] == patch)

    def not_me(device):
        return (device[0] != frame) | (device[1] != patch)

    def target1(i):
        xt = rem(x + div(i, 8), 4)
        ct = rem(c + 1 + i, 4)
        kt = rem(div(i, 4), 2)
        zt = 2 * ct + flip(zh, ct)
        return (xt * 8 + rem(zt, 4) * 2 + kt, div(zt, 4) * 4 + y), ct, kt * 4 + xt

    def source1(i):
        return (i, pg_src)

    def target2(f):
        zt = 2 * c + rem(f, 2)
        return (div(f, 8) * 8 + rem(zt, 4) * 2 + core, div(zt, 4) * 4 + rem(div(f, 2), 4))

    def source2(i):
        zs = 2 * c + rem(i, 2)
        return (div(i, 8) * 8 + rem(zs, 4) * 2 + core, div(zs, 4) * 4 + rem(div(i, 2), 4))

    home_frame = x * 8 + y * 2 + zb

    def target4(g):
        return (home_frame, g)

    def source4(i):
        zs = 2 * div(i, 2) + core
        return (x * 8 + rem(zs, 4) * 2 + rem(i, 2), div(zs, 4) * 4 + zl)

    partner = (x * 8 + zl * 2 + 1 - core, patch)

    loads = (
        pltpu.make_async_copy(w_tqkv, wt, wsem.at[0]),
        pltpu.make_async_copy(w_out, wo, wsem.at[1]),
        pltpu.make_async_copy(w_sqkv, ws, wsem.at[2]),
    )
    loads[0].start()
    loads[1].start()
    loads[2].start()

    barrier = pltpu.get_barrier_semaphore()

    def greet(device):
        @pl.when(not_me(device))
        def _():
            pl.semaphore_signal(barrier, inc=1, device_id=device, device_id_type=MESH)

    def greet1(i, carry):
        greet(source1(rem(frame + i, 32)))
        return carry

    def greet2(i, carry):
        greet(source2(i))
        return carry

    def greet4(i, carry):
        greet(source4(i))
        return carry

    lax.fori_loop(0, 32, greet1, 0)
    lax.fori_loop(0, 32, greet2, 0)
    lax.fori_loop(0, 8, greet4, 0)
    greet(partner)

    rows = lax.broadcasted_iota(jnp.int32, (INNER, INNER), 0)
    cols = lax.broadcasted_iota(jnp.int32, (INNER, INNER), 1)
    head_of = lambda v: lax.shift_right_logical(v * 52429, 22)
    blocks[...] = jnp.where(head_of(rows) == head_of(cols), 1.0, 0.0).astype(BF)
    rows = lax.broadcasted_iota(jnp.int32, (128, 512), 0)
    cols = lax.broadcasted_iota(jnp.int32, (128, 512), 1)
    pmask[...] = jnp.where((rows & 15) == (cols & 15), 1.0, 0.0).astype(BF)

    own1 = jnp.where(zh_src == zh, 1, 0)
    own4 = jnp.where((core == zb) & (zl == y), 1, 0)
    pl.semaphore_wait(barrier, 32 - own1 + 31 + 8 - own4 + 1)

    def copy1(i):
        device, ct, b = target1(i)
        src = clip.at[ct, 0, pl.ds(pl.multiple_of(b * 16, 16), 16)]
        return device, src

    def send1(i, carry):
        device, src = copy1(i)

        @pl.when(not_me(device))
        def _():
            pltpu.make_async_remote_copy(
                src_ref=src, dst_ref=tok.at[frame], send_sem=s1.at[i], recv_sem=r1.at[frame],
                device_id=device, device_id_type=MESH,
            ).start()

        @pl.when(is_me(device))
        def _():
            pltpu.make_async_copy(src, tok.at[frame], r1.at[frame]).start()

        return carry

    lax.fori_loop(0, 32, send1, 0)

    def layer_norm(values, gain):
        average = jnp.mean(values, axis=-1, keepdims=True)
        centred = values - average
        variance = jnp.mean(centred * centred, axis=-1, keepdims=True)
        return (centred * lax.rsqrt(variance + EPS) * gain).astype(BF)

    def head_norm(part, gain):
        squares = jnp.dot((part * part).astype(BF), blocks[...], preferred_element_type=F32)
        return (part * lax.rsqrt(squares * (1.0 / HDIM) + EPS) * gain).astype(BF)

    def project(values, norm, weight, q_gain, k_gain):
        normed = layer_norm(values, norm[...])
        product = jnp.dot(normed, weight[...], preferred_element_type=F32)
        query = head_norm(product[:, :INNER], q_gain[...])
        keys = head_norm(product[:, INNER : 2 * INNER], k_gain[...])
        return query, keys, product[:, 2 * INNER :].astype(BF)

    def wait_local(src, dst, sem):
        pltpu.make_async_copy(src, dst, sem).wait()

    loads[0].wait()

    def time_project(j, carry):
        xs = rem(x + j, 4)

        def wait(i, inner):
            slot = xs * 8 + i
            wait_local(tok.at[slot], tok.at[slot], r1.at[slot])
            return inner

        lax.fori_loop(0, 8, wait, 0)
        values = tok[pl.ds(xs * 8, 8)].reshape(128, D).astype(F32)
        query, keys, vals = project(values, norm_t, wt, qg_t, kg_t)
        tq[xs] = query
        at = pl.ds(pl.multiple_of(xs * 128, 128), 128)
        tk[at, :] = keys
        tv[at, :] = vals
        return carry

    lax.fori_loop(0, 4, time_project, 0)
    loads[1].wait()

    lane = lax.broadcasted_iota(jnp.int32, (1, 256), 1)

    def time_attend(j, carry):
        xs = rem(x + 1 + j, 4)
        tiles = [jnp.zeros((128, 128), F32)] * 5
        for h in range(HEADS):
            w = WINDOWS[h]
            first = h * HDIM - w
            mask = (lane >= first) & (lane < first + HDIM)
            spare = 255 if first + HDIM <= 255 else 0
            query = jnp.where(mask, tq[xs, :, w : w + 256], 0.0).astype(BF)
            scores = lax.dot_general(
                query, tk[:, w : w + 256], (((1,), (1,)), ((), ())), preferred_element_type=F32
            )
            prob = jnp.exp2(scores * SCALE).astype(BF) * pmask[...]
            vals = jnp.where(mask, tv[:, w : w + 256], 1.0).astype(BF)
            summed = jnp.dot(prob, vals, preferred_element_type=F32)
            result = summed * (1.0 / summed[:, spare : spare + 1])
            t = w // 128
            tiles[t] = jnp.where(mask[:, :128], result[:, :128], tiles[t])
            tiles[t + 1] = jnp.where(mask[:, 128:], result[:, 128:], tiles[t + 1])
        attended = jnp.concatenate([tile.astype(BF) for tile in tiles], axis=1)
        delta = jnp.dot(attended, wo[...], preferred_element_type=F32)
        values = tok[pl.ds(xs * 8, 8)].reshape(128, D).astype(F32)
        mixed[pl.ds(xs * 8, 8)] = (values + delta).astype(BF).reshape(8, 16, D)

        def send(i, inner):
            f = xs * 8 + i
            device = target2(f)
            slot = x * 8 + pg_src

            @pl.when(not_me(device))
            def _():
                pltpu.make_async_remote_copy(
                    src_ref=mixed.at[f], dst_ref=tok2.at[slot], send_sem=s2.at[f],
                    recv_sem=r2.at[slot], device_id=device, device_id_type=MESH,
                ).start()

            @pl.when(is_me(device))
            def _():
                pltpu.make_async_copy(mixed.at[f], tok2.at[slot], r2.at[slot]).start()

            return inner

        lax.fori_loop(0, 8, send, 0)
        return carry

    lax.fori_loop(0, 4, time_attend, 0)
    loads[2].wait()

    def exchange(xs):
        return pltpu.make_async_remote_copy(
            src_ref=send_qkv.at[xs], dst_ref=qkv.at[core, xs], send_sem=sq.at[xs],
            recv_sem=rq.at[xs], device_id=partner, device_id_type=MESH,
        )

    def space_project(j, carry):
        xs = rem(x + 3 - j, 4)

        def wait(i, inner):
            slot = xs * 8 + i
            wait_local(tok2.at[slot], tok2.at[slot], r2.at[slot])
            return inner

        lax.fori_loop(0, 8, wait, 0)
        values = tok2[pl.ds(xs * 8, 8)].reshape(128, D).astype(F32)
        parts = project(values, norm_s, ws, qg_s, kg_s)
        for n in range(3):
            low, high = parts[n][:, :HALF], parts[n][:, INNER - HALF :]
            qkv[core, xs, n] = jnp.where(core == 0, low, high).reshape(8, 16, HALF)
            send_qkv[xs, n] = jnp.where(core == 0, high, low).reshape(8, 16, HALF)
        exchange(xs).start()
        return carry

    lax.fori_loop(0, 4, space_project, 0)

    def wait_partner(xs, carry):
        wait_local(send_qkv.at[xs], qkv.at[1 - core, xs], rq.at[xs])
        return carry

    lax.fori_loop(0, 4, wait_partner, 0)

    def head_mask(j):
        first = j * HDIM + 64 * core - (0 if j < 2 else 128)
        return (lane >= first) & (lane < first + HDIM)

    for j in range(4):
        w = 0 if j < 2 else 128
        vals = qkv[:, :, 2, :, :, w : w + 256].reshape(1024, 256)
        vm[j] = jnp.where(head_mask(j), vals, 1.0).astype(BF)

    def send4(g):
        device = target4(g)
        slot = c * 2 + core
        src, dst = att.at[g], home.at[slot]

        @pl.when(not_me(device))
        def _():
            pltpu.make_async_remote_copy(
                src_ref=src, dst_ref=dst, send_sem=s4.at[g], recv_sem=r4.at[slot],
                device_id=device, device_id_type=MESH,
            ).start()

        @pl.when(is_me(device))
        def _():
            pltpu.make_async_copy(src, dst, r4.at[slot]).start()

    def space_attend(j, carry):
        t = rem(zl + j, 4)
        tiles = [jnp.zeros((256, 128), F32)] * 3
        for h in range(4):
            w = 0 if h < 2 else 128
            spare = 255 if h < 2 else 0
            mask = head_mask(h)
            query = qkv[:, :, 0, pl.ds(2 * t, 2), :, w : w + 256].reshape(256, 256)
            query = jnp.where(mask, query, 0.0).astype(BF)
            keys = qkv[:, :, 1, :, :, w : w + 256].reshape(1024, 256)
            scores = lax.dot_general(
                query, keys, (((1,), (1,)), ((), ())), preferred_element_type=F32
            )
            prob = jnp.exp2(scores * SCALE).astype(BF)
            summed = jnp.dot(prob, vm[h], preferred_element_type=F32)
            result = summed * (1.0 / summed[:, spare : spare + 1])
            n = w // 128
            tiles[n] = jnp.where(mask[:, :128], result[:, :128], tiles[n])
            tiles[n + 1] = jnp.where(mask[:, 128:], result[:, 128:], tiles[n + 1])
        for n in range(3):
            tile = tiles[n].astype(BF).reshape(8, 2, 16, 128)
            for g in range(2):
                att[2 * t + g, :, :, n * 128 : (n + 1) * 128] = tile[:, g]
        send4(2 * t)
        send4(2 * t + 1)
        return carry

    lax.fori_loop(0, 4, space_attend, 0)

    def finish(i, carry):
        wait_local(home.at[2 * i], home.at[2 * i], r4.at[2 * i])
        wait_local(home.at[2 * i + 1], home.at[2 * i + 1], r4.at[2 * i + 1])
        low, high = home[2 * i].reshape(128, HALF), home[2 * i + 1].reshape(128, HALF)
        out[i, 0, :, :256] = low[:, :256]
        out[i, 0, :, 256:384] = low[:, 256:] + high[:, :128]
        out[i, 0, :, 384:] = high[:, 128:]
        return carry

    lax.fori_loop(0, 4, finish, 0)

    def done1(i, carry):
        device, src = copy1(i)

        @pl.when(not_me(device))
        def _():
            pltpu.make_async_remote_copy(
                src_ref=src, dst_ref=tok.at[frame], send_sem=s1.at[i], recv_sem=r1.at[frame],
                device_id=device, device_id_type=MESH,
            ).wait_send()

        return carry

    def done2(f, carry):
        device = target2(f)

        @pl.when(not_me(device))
        def _():
            pltpu.make_async_remote_copy(
                src_ref=mixed.at[f], dst_ref=tok2.at[f], send_sem=s2.at[f], recv_sem=r2.at[f],
                device_id=device, device_id_type=MESH,
            ).wait_send()

        return carry

    def done3(xs, carry):
        exchange(xs).wait_send()
        return carry

    def done4(g, carry):
        device = target4(g)

        @pl.when(not_me(device))
        def _():
            pltpu.make_async_remote_copy(
                src_ref=att.at[g], dst_ref=home.at[0], send_sem=s4.at[g], recv_sem=r4.at[0],
                device_id=device, device_id_type=MESH,
            ).wait_send()

        return carry

    lax.fori_loop(0, 32, done1, 0)
    lax.fori_loop(0, 32, done2, 0)
    lax.fori_loop(0, 4, done3, 0)
    lax.fori_loop(0, 8, done4, 0)


def body(
    clip, norm_time, w_time_qkv, q_gain_time, k_gain_time, w_time_out,
    norm_space, w_space_qkv, q_gain_space, k_gain_space,
):
    anywhere = pl.BlockSpec(memory_space=pl.ANY)
    vmem = pl.BlockSpec(memory_space=pltpu.VMEM)
    dma = pltpu.SemaphoreType.DMA
    flat = lambda gain: gain.reshape(1, -1)
    return pl.pallas_call(
        kernel,
        out_shape=jax.ShapeDtypeStruct((4, 1, 128, INNER), BF),
        in_specs=[anywhere, vmem, anywhere, vmem, vmem, anywhere, vmem, anywhere, vmem, vmem],
        out_specs=vmem,
        scratch_shapes=[
            pltpu.VMEM((D, 3 * INNER), BF),
            pltpu.VMEM((INNER, D), BF),
            pltpu.VMEM((D, 3 * INNER), BF),
            pltpu.VMEM((INNER, INNER), BF),
            pltpu.VMEM((128, 512), BF),
            pltpu.VMEM((32, 16, D), BF),
            pltpu.VMEM((4, 128, INNER), BF),
            pltpu.VMEM((512, INNER), BF),
            pltpu.VMEM((512, INNER), BF),
            pltpu.VMEM((32, 16, D), BF),
            pltpu.VMEM((32, 16, D), BF),
            pltpu.VMEM((4, 3, 8, 16, HALF), BF),
            pltpu.VMEM((2, 4, 3, 8, 16, HALF), BF),
            pltpu.VMEM((4, 1024, 256), BF),
            pltpu.VMEM((8, 8, 16, HALF), BF),
            pltpu.VMEM((8, 8, 16, HALF), BF),
            dma((3,)),
            dma((32,)), dma((32,)),
            dma((32,)), dma((32,)),
            dma((4,)), dma((4,)),
            dma((8,)), dma((8,)),
        ],
        compiler_params=pltpu.CompilerParams(
            collective_id=0, has_side_effects=True, vmem_limit_bytes=58 * 2**20
        ),
        cost_estimate=pl.CostEstimate(
            flops=2 * 512 * D * (6 * INNER + INNER), bytes_accessed=14 * 2**20, transcendentals=6 * 2**20
        ),
    )(
        clip, flat(norm_time), w_time_qkv, flat(q_gain_time), flat(k_gain_time), w_time_out,
        flat(norm_space), w_space_qkv, flat(q_gain_space), flat(k_gain_space),
    )


def solution(mesh):
    in_specs = (P(None, "frame", "patch", None),) + (P(),) * 9
    out_specs = P(None, "frame", "patch", None)
    return jax.shard_map(body, mesh=mesh, in_specs=in_specs, out_specs=out_specs, check_vma=False)
```

time: 443 us -> 126 us (0.28)
  the two profiles are of different devices: /device:TPU:1 before, /device:TPU:65 now
where the time goes in v1:
time: 126 us
  Pallas kernels  116 us (92%)
  local copies, waits for them, and re-layouts  9.61 us (8%)
    pallas_call x1, Pallas kernels, body(): pl.pallas_call(kernel, out_shape=jax.ShapeDtypeStruct((4, 1, 128, INNER),...  116 us
    reshape x6, local copies, waits for them, and re-layouts, body(): flat = lambda gain: gain.reshape(1, -1)  7.63 us

profile of v1, /device:TPU:65, one launch (start us, length us, event | category | flops | bytes accessed | tf_op | source)
XLA Modules:
  0.0 126.1 jit_solution(16633915295305941809)
XLA Ops:
  0.0 1.3 %reshape.19.qg_t = f32[1,640]{1,0:T(1,128)} reshape(f32[640]{0:T(1024)} %param.13) | data formatting | bytes 5120 | tf_op jit(solution)/shard_map/reshape | solution.py:394
  1.3 1.3 reshape.20.kg_t
  2.5 1.3 %reshape.22.qg_s = f32[1,640]{1,0:T(1,128)} reshape(f32[640]{0:T(1024)} %param.18) | data formatting | bytes 5120 | tf_op jit(solution)/shard_map/reshape | solution.py:394
  3.8 1.3 %reshape.23.kg_s = f32[1,640]{1,0:T(1,128)} reshape(f32[640]{0:T(1024)} %param.19) | data formatting | bytes 5120 | tf_op jit(solution)/shard_map/reshape | solution.py:394
  5.1 1.3 %reshape.18.norm_t = f32[1,1280]{1,0:T(1,128)} reshape(f32[1280]{0:T(1024)} %param.11) | data formatting | bytes 10240 | tf_op jit(solution)/shard_map/reshape | solution.py:394
  6.4 1.3 %reshape.21.norm_s = f32[1,1280]{1,0:T(1,128)} reshape(f32[1280]{0:T(1024)} %param.16) | data formatting | bytes 10240 | tf_op jit(solution)/shard_map/reshape | solution.py:394
  7.6 116.5 %shard_map.100 = bf16[4,1,128,640]{3,2,1,0:T(8,128)(2,1)} custom-call(bf16[4,1,128,1280]{3,2,1,0:T(8,128)(2,1)} %clip.1, f32[1,1280]{1,0:T(1,128)} %reshape.18.norm_t, bf16[1280,1920]{1,0:T(8,128)(2,1)} %w_tqkv.1, f32[1,640]{1,0:T(1,128)} %reshape.19.qg_t, f32[1,640]{1,0:T(1,128)} %reshape.20.kg_t, bf16[640,1280]{1,0:T(8,128)(2,1)} %w_out.1, ...), custom_call_target="tpu_custom_call" | custom-call | flops 5872025600 | bytes 14680064 | tf_op jit(solution)/shard_map/pallas_call | solution.py:395
  124.1 2.0 %copy.12 = bf16[4,1,128,640]{3,2,1,0:T(8,128)(2,1)} copy(bf16[4,1,128,640]{3,2,1,0:T(8,128)(2,1)} %shard_map.100) | data formatting | bytes 1310720

commit v2 on v1

--- a/solution.py
+++ b/solution.py
@@ -31,7 +31,7 @@
 def kernel(
     clip, norm_t, w_tqkv, qg_t, kg_t, w_out, norm_s, w_sqkv, qg_s, kg_s,
     out,
-    wt, wo, ws, blocks, pmask, tok, tq, tk, tv, mixed, tok2, send_qkv, qkv, vm, att, home,
+    wt, wo, ws, blocks, pmask, swap, tok, tq, tk, tv, tatt, mixed, tok2, send_qkv, qkv, vm, att, home,
     wsem, s1, r1, s2, r2, sq, rq, s4, r4,
 ):
     frame, patch = lax.axis_index("frame"), lax.axis_index("patch")
@@ -64,20 +64,22 @@
 
     def target2(f):
         zt = 2 * c + rem(f, 2)
-        return (div(f, 8) * 8 + rem(zt, 4) * 2 + core, div(zt, 4) * 4 + rem(div(f, 2), 4))
+        yt = rem(div(f, 2) + zt, 4)
+        return (div(f, 8) * 8 + rem(zt, 4) * 2 + core, div(zt, 4) * 4 + yt)
 
     def source2(i):
         zs = 2 * c + rem(i, 2)
         return (div(i, 8) * 8 + rem(zs, 4) * 2 + core, div(zs, 4) * 4 + rem(div(i, 2), 4))
 
-    home_frame = x * 8 + y * 2 + zb
+    home_zl = rem(y + 8 - z, 4)
+    home_frame = x * 8 + home_zl * 2 + zb
 
     def target4(g):
         return (home_frame, g)
 
     def source4(i):
         zs = 2 * div(i, 2) + core
-        return (x * 8 + rem(zs, 4) * 2 + rem(i, 2), div(zs, 4) * 4 + zl)
+        return (x * 8 + rem(zs, 4) * 2 + rem(i, 2), div(zs, 4) * 4 + rem(zl + zs, 4))
 
     partner = (x * 8 + zl * 2 + 1 - core, patch)
 
@@ -118,12 +120,13 @@
     cols = lax.broadcasted_iota(jnp.int32, (INNER, INNER), 1)
     head_of = lambda v: lax.shift_right_logical(v * 52429, 22)
     blocks[...] = jnp.where(head_of(rows) == head_of(cols), 1.0, 0.0).astype(BF)
-    rows = lax.broadcasted_iota(jnp.int32, (128, 512), 0)
-    cols = lax.broadcasted_iota(jnp.int32, (128, 512), 1)
-    pmask[...] = jnp.where((rows & 15) == (cols & 15), 1.0, 0.0).astype(BF)
+    rows = lax.broadcasted_iota(jnp.int32, (128, 128), 0)
+    cols = lax.broadcasted_iota(jnp.int32, (128, 128), 1)
+    pmask[...] = jnp.where((rows >> 5) == (cols >> 5), 1.0, 0.0).astype(BF)
+    swap[...] = jnp.where(cols == (rows & 7) * 16 + (rows >> 3), 1.0, 0.0).astype(BF)
 
     own1 = jnp.where(zh_src == zh, 1, 0)
-    own4 = jnp.where((core == zb) & (zl == y), 1, 0)
+    own4 = jnp.where(home_frame == frame, 1, 0)
     pl.semaphore_wait(barrier, 32 - own1 + 31 + 8 - own4 + 1)
 
     def copy1(i):
@@ -180,12 +183,13 @@
             return inner
 
         lax.fori_loop(0, 8, wait, 0)
-        values = tok[pl.ds(xs * 8, 8)].reshape(128, D).astype(F32)
-        query, keys, vals = project(values, norm_t, wt, qg_t, kg_t)
-        tq[xs] = query
-        at = pl.ds(pl.multiple_of(xs * 128, 128), 128)
-        tk[at, :] = keys
-        tv[at, :] = vals
+        values = jnp.dot(
+            swap[...], tok[pl.ds(xs * 8, 8)].reshape(128, D), preferred_element_type=F32
+        )
+        parts = project(values, norm_t, wt, qg_t, kg_t)
+        at = pl.ds(pl.multiple_of(xs * 8, 8), 8)
+        for ref, part in zip((tq, tk, tv), parts):
+            ref[:, at, :] = part.astype(F32).reshape(16, 8, INNER)
         return carry
 
     lax.fori_loop(0, 4, time_project, 0)
@@ -193,32 +197,52 @@
 
     lane = lax.broadcasted_iota(jnp.int32, (1, 256), 1)
 
-    def time_attend(j, carry):
-        xs = rem(x + 1 + j, 4)
+    def time_attend(g, carry):
+        at = pl.ds(4 * g, 4)
         tiles = [jnp.zeros((128, 128), F32)] * 5
         for h in range(HEADS):
             w = WINDOWS[h]
             first = h * HDIM - w
             mask = (lane >= first) & (lane < first + HDIM)
             spare = 255 if first + HDIM <= 255 else 0
-            query = jnp.where(mask, tq[xs, :, w : w + 256], 0.0).astype(BF)
+            query = jnp.where(mask, tq[at, :, w : w + 256].reshape(128, 256), 0.0).astype(BF)
+            keys = tk[at, :, w : w + 256].reshape(128, 256).astype(BF)
             scores = lax.dot_general(
-                query, tk[:, w : w + 256], (((1,), (1,)), ((), ())), preferred_element_type=F32
+                query, keys, (((1,), (1,)), ((), ())), preferred_element_type=F32
             )
             prob = jnp.exp2(scores * SCALE).astype(BF) * pmask[...]
-            vals = jnp.where(mask, tv[:, w : w + 256], 1.0).astype(BF)
+            vals = jnp.where(mask, tv[at, :, w : w + 256].reshape(128, 256), 1.0).astype(BF)
             summed = jnp.dot(prob, vals, preferred_element_type=F32)
             result = summed * (1.0 / summed[:, spare : spare + 1])
             t = w // 128
             tiles[t] = jnp.where(mask[:, :128], result[:, :128], tiles[t])
             tiles[t + 1] = jnp.where(mask[:, 128:], result[:, 128:], tiles[t + 1])
-        attended = jnp.concatenate([tile.astype(BF) for tile in tiles], axis=1)
+        rows = pl.ds(pl.multiple_of(g * 128, 128), 128)
+        for n in range(5):
+            tatt[rows, n * 128 : (n + 1) * 128] = tiles[n].astype(BF)
+        return carry
+
+    lax.fori_loop(0, 4, time_attend, 0)
+
+    def time_mix(j, carry):
+        zls = [rem(x + j + 4 - a, 4) for a in range(4)]
+        first = [a * 8 + zls[a] * 2 for a in range(4)]
+        parts = []
+        for a in range(4):
+            rows = lax.broadcasted_iota(jnp.int32, (32, 512), 0)
+            cols = lax.broadcasted_iota(jnp.int32, (32, 512), 1)
+            parts.append(cols == (rows & 15) * 32 + (rows >> 4) + first[a])
+        pick = jnp.concatenate([jnp.where(part, 1.0, 0.0).astype(BF) for part in parts], axis=0)
+        attended = jnp.dot(pick, tatt[...], preferred_element_type=F32).astype(BF)
         delta = jnp.dot(attended, wo[...], preferred_element_type=F32)
-        values = tok[pl.ds(xs * 8, 8)].reshape(128, D).astype(F32)
-        mixed[pl.ds(xs * 8, 8)] = (values + delta).astype(BF).reshape(8, 16, D)
+        for a in range(4):
+            values = tok[pl.ds(first[a], 2)].reshape(32, D).astype(F32)
+            total = (values + delta[32 * a : 32 * a + 32]).astype(BF)
+            mixed[pl.ds(first[a], 2)] = total.reshape(2, 16, D)
 
         def send(i, inner):
-            f = xs * 8 + i
+            a = rem(x + 1 + i, 4)
+            f = a * 8 + rem(x + j + 4 - a, 4) * 2 + div(i, 4)
             device = target2(f)
             slot = x * 8 + pg_src
 
@@ -238,7 +262,7 @@
         lax.fori_loop(0, 8, send, 0)
         return carry
 
-    lax.fori_loop(0, 4, time_attend, 0)
+    lax.fori_loop(0, 4, time_mix, 0)
     loads[2].wait()
 
     def exchange(xs):
@@ -248,7 +272,7 @@
         )
 
     def space_project(j, carry):
-        xs = rem(x + 3 - j, 4)
+        xs = rem(x + home_zl + 4 - j, 4)
 
         def wait(i, inner):
             slot = xs * 8 + i
@@ -317,10 +341,15 @@
             n = w // 128
             tiles[n] = jnp.where(mask[:, :128], result[:, :128], tiles[n])
             tiles[n + 1] = jnp.where(mask[:, 128:], result[:, 128:], tiles[n + 1])
-        for n in range(3):
-            tile = tiles[n].astype(BF).reshape(8, 2, 16, 128)
-            for g in range(2):
-                att[2 * t + g, :, :, n * 128 : (n + 1) * 128] = tile[:, g]
+        first = core == 0
+        whole = [jnp.where(first, tiles[n], tiles[n + 1]).astype(BF) for n in range(2)]
+        shared = jnp.where(first, tiles[2], tiles[0])
+        packed = shared[:128] + pltpu.roll(shared[128:], 64, 1)
+        packed = packed.astype(BF).reshape(4, 2, 16, 128)
+        for g in range(2):
+            for n in range(2):
+                att[2 * t + g, 8 * n : 8 * n + 8] = whole[n].reshape(8, 2, 16, 128)[:, g]
+            att[2 * t + g, 16:] = packed[:, g]
         send4(2 * t)
         send4(2 * t + 1)
         return carry
@@ -330,10 +359,15 @@
     def finish(i, carry):
         wait_local(home.at[2 * i], home.at[2 * i], r4.at[2 * i])
         wait_local(home.at[2 * i + 1], home.at[2 * i + 1], r4.at[2 * i + 1])
-        low, high = home[2 * i].reshape(128, HALF), home[2 * i + 1].reshape(128, HALF)
-        out[i, 0, :, :256] = low[:, :256]
-        out[i, 0, :, 256:384] = low[:, 256:] + high[:, :128]
-        out[i, 0, :, 384:] = high[:, 128:]
+        for half in range(2):
+            for n in range(2):
+                at = (3 * half + n) * 128
+                out[i, 0, :, at : at + 128] = home[2 * i + half, 8 * n : 8 * n + 8].reshape(128, 128)
+        low = home[2 * i, 16:].reshape(64, 128).astype(F32)
+        high = home[2 * i + 1, 16:].reshape(64, 128).astype(F32)
+        left = lane[:, :128] < 64
+        out[i, 0, :64, 256:384] = jnp.where(left, low, high).astype(BF)
+        out[i, 0, 64:, 256:384] = pltpu.roll(jnp.where(left, high, low), 64, 1).astype(BF)
         return carry
 
     lax.fori_loop(0, 4, finish, 0)
@@ -402,18 +436,20 @@
             pltpu.VMEM((INNER, D), BF),
             pltpu.VMEM((D, 3 * INNER), BF),
             pltpu.VMEM((INNER, INNER), BF),
-            pltpu.VMEM((128, 512), BF),
+            pltpu.VMEM((128, 128), BF),
+            pltpu.VMEM((128, 128), BF),
             pltpu.VMEM((32, 16, D), BF),
-            pltpu.VMEM((4, 128, INNER), BF),
-            pltpu.VMEM((512, INNER), BF),
+            pltpu.VMEM((16, 32, INNER), F32),
+            pltpu.VMEM((16, 32, INNER), F32),
+            pltpu.VMEM((16, 32, INNER), F32),
             pltpu.VMEM((512, INNER), BF),
             pltpu.VMEM((32, 16, D), BF),
             pltpu.VMEM((32, 16, D), BF),
             pltpu.VMEM((4, 3, 8, 16, HALF), BF),
             pltpu.VMEM((2, 4, 3, 8, 16, HALF), BF),
             pltpu.VMEM((4, 1024, 256), BF),
-            pltpu.VMEM((8, 8, 16, HALF), BF),
-            pltpu.VMEM((8, 8, 16, HALF), BF),
+            pltpu.VMEM((8, 20, 16, 128), BF),
+            pltpu.VMEM((8, 20, 16, 128), BF),
             dma((3,)),
             dma((32,)), dma((32,)),
             dma((32,)), dma((32,)),

time: 126 us -> 112 us (0.89)
  the two profiles are of different devices: /device:TPU:65 before, /device:TPU:1 now
where the time goes in v2:
time: 112 us; the launch traced here: 110 us
  Pallas kernels  100 us (89%)
  local copies, waits for them, and re-layouts  9.61 us (9%)
    pallas_call x1, Pallas kernels, body(): pl.pallas_call(kernel, out_shape=jax.ShapeDtypeStruct((4, 1, 128, INNER),...  100 us
    reshape x6, local copies, waits for them, and re-layouts, body(): flat = lambda gain: gain.reshape(1, -1)  7.63 us

profile of v2, /device:TPU:1, one launch (start us, length us, event | category | flops | bytes accessed | tf_op | source)
XLA Modules:
  0.0 109.8 jit_solution(16813562415551461815)
XLA Ops:
  0.0 1.3 %reshape.19.qg_t = f32[1,640]{1,0:T(1,128)} reshape(f32[640]{0:T(1024)} %param.13) | data formatting | bytes 5120 | tf_op jit(solution)/shard_map/reshape | solution.py:428
  1.3 1.3 %reshape.20.kg_t = f32[1,640]{1,0:T(1,128)} reshape(f32[640]{0:T(1024)} %param.14) | data formatting | bytes 5120 | tf_op jit(solution)/shard_map/reshape | solution.py:428
  2.5 1.3 %reshape.22.qg_s = f32[1,640]{1,0:T(1,128)} reshape(f32[640]{0:T(1024)} %param.18) | data formatting | bytes 5120 | tf_op jit(solution)/shard_map/reshape | solution.py:428
  3.8 1.3 %reshape.23.kg_s = f32[1,640]{1,0:T(1,128)} reshape(f32[640]{0:T(1024)} %param.19) | data formatting | bytes 5120 | tf_op jit(solution)/shard_map/reshape | solution.py:428
  5.1 1.3 %reshape.18.norm_t = f32[1,1280]{1,0:T(1,128)} reshape(f32[1280]{0:T(1024)} %param.11) | data formatting | bytes 10240 | tf_op jit(solution)/shard_map/reshape | solution.py:428
  6.4 1.3 %reshape.21.norm_s = f32[1,1280]{1,0:T(1,128)} reshape(f32[1280]{0:T(1024)} %param.16) | data formatting | bytes 10240 | tf_op jit(solution)/shard_map/reshape | solution.py:428
  7.6 100.2 %shard_map.100 = bf16[4,1,128,640]{3,2,1,0:T(8,128)(2,1)} custom-call(bf16[4,1,128,1280]{3,2,1,0:T(8,128)(2,1)} %clip.1, f32[1,1280]{1,0:T(1,128)} %reshape.18.norm_t, bf16[1280,1920]{1,0:T(8,128)(2,1)} %w_tqkv.1, f32[1,640]{1,0:T(1,128)} %reshape.19.qg_t, f32[1,640]{1,0:T(1,128)} %reshape.20.kg_t, bf16[640,1280]{1,0:T(8,128)(2,1)} %w_out.1, ...), custom_call_target="tpu_custom_call" | custom-call | flops 5872025600 | bytes 14680064 | tf_op jit(solution)/shard_map/pallas_call | solution.py:429
  107.8 2.0 %copy.12 = bf16[4,1,128,640]{3,2,1,0:T(8,128)(2,1)} copy(bf16[4,1,128,640]{3,2,1,0:T(8,128)(2,1)} %shard_map.100) | data formatting | bytes 1310720

commit v3 on v2

--- a/solution.py
+++ b/solution.py
@@ -30,8 +30,8 @@
 
 def kernel(
     clip, norm_t, w_tqkv, qg_t, kg_t, w_out, norm_s, w_sqkv, qg_s, kg_s,
-    out,
-    wt, wo, ws, blocks, pmask, swap, tok, tq, tk, tv, tatt, mixed, tok2, send_qkv, qkv, vm, att, home,
+    home,
+    wt, wo, ws, blocks, pmask, swap, tok, tq, tk, tv, tatt, mixed, tok2, send_qkv, qkv, vm, att,
     wsem, s1, r1, s2, r2, sq, rq, s4, r4,
 ):
     frame, patch = lax.axis_index("frame"), lax.axis_index("patch")
@@ -53,7 +53,7 @@
         return (device[0] != frame) | (device[1] != patch)
 
     def target1(i):
-        xt = rem(x + div(i, 8), 4)
+        xt = rem(x + zl + 4 - div(i, 8), 4)
         ct = rem(c + 1 + i, 4)
         kt = rem(div(i, 4), 2)
         zt = 2 * ct + flip(zh, ct)
@@ -64,14 +64,14 @@
 
     def target2(f):
         zt = 2 * c + rem(f, 2)
-        yt = rem(div(f, 2) + zt, 4)
+        yt = rem(div(f, 2) + c + 2 * rem(f, 2), 4)
         return (div(f, 8) * 8 + rem(zt, 4) * 2 + core, div(zt, 4) * 4 + yt)
 
     def source2(i):
         zs = 2 * c + rem(i, 2)
         return (div(i, 8) * 8 + rem(zs, 4) * 2 + core, div(zs, 4) * 4 + rem(div(i, 2), 4))
 
-    home_zl = rem(y + 8 - z, 4)
+    home_zl = rem(y + 8 - c - 2 * zb, 4)
     home_frame = x * 8 + home_zl * 2 + zb
 
     def target4(g):
@@ -79,7 +79,7 @@
 
     def source4(i):
         zs = 2 * div(i, 2) + core
-        return (x * 8 + rem(zs, 4) * 2 + rem(i, 2), div(zs, 4) * 4 + rem(zl + zs, 4))
+        return (x * 8 + rem(zs, 4) * 2 + rem(i, 2), div(zs, 4) * 4 + rem(zl + div(i, 2) + 2 * core, 4))
 
     partner = (x * 8 + zl * 2 + 1 - core, patch)
 
@@ -150,7 +150,7 @@
 
         return carry
 
-    lax.fori_loop(0, 32, send1, 0)
+    lax.fori_loop(0, 16, send1, 0)
 
     def layer_norm(values, gain):
         average = jnp.mean(values, axis=-1, keepdims=True)
@@ -163,10 +163,10 @@
         return (part * lax.rsqrt(squares * (1.0 / HDIM) + EPS) * gain).astype(BF)
 
     def project(values, norm, weight, q_gain, k_gain):
-        normed = layer_norm(values, norm[...])
+        normed = layer_norm(values, norm[...].reshape(1, -1))
         product = jnp.dot(normed, weight[...], preferred_element_type=F32)
-        query = head_norm(product[:, :INNER], q_gain[...])
-        keys = head_norm(product[:, INNER : 2 * INNER], k_gain[...])
+        query = head_norm(product[:, :INNER], q_gain[...].reshape(1, -1))
+        keys = head_norm(product[:, INNER : 2 * INNER], k_gain[...].reshape(1, -1))
         return query, keys, product[:, 2 * INNER :].astype(BF)
 
     def wait_local(src, dst, sem):
@@ -174,20 +174,37 @@
 
     loads[0].wait()
 
+    def sent1(i, carry):
+        device, src = copy1(i)
+
+        @pl.when(not_me(device))
+        def _():
+            pltpu.make_async_remote_copy(
+                src_ref=src, dst_ref=tok.at[frame], send_sem=s1.at[i], recv_sem=r1.at[frame],
+                device_id=device, device_id_type=MESH,
+            ).wait_send()
+
+        return carry
+
+    def pairs_of(d):
+        return [a * 8 + rem(d + 4 - a, 4) * 2 for a in range(4)]
+
     def time_project(j, carry):
-        xs = rem(x + j, 4)
-
-        def wait(i, inner):
-            slot = xs * 8 + i
-            wait_local(tok.at[slot], tok.at[slot], r1.at[slot])
-            return inner
-
-        lax.fori_loop(0, 8, wait, 0)
-        values = jnp.dot(
-            swap[...], tok[pl.ds(xs * 8, 8)].reshape(128, D), preferred_element_type=F32
-        )
+        @pl.when(j < 2)
+        def _():
+            lax.fori_loop(0, 8, lambda i, inner: sent1(8 * j + i, inner), 0)
+            lax.fori_loop(0, 8, lambda i, inner: send1(8 * j + 16 + i, inner), 0)
+
+        d = rem(x + j, 4)
+        first = pairs_of(d)
+        for a in range(4):
+            for k in range(2):
+                slot = first[a] + k
+                wait_local(tok.at[slot], tok.at[slot], r1.at[slot])
+        values = jnp.concatenate([tok[pl.ds(f, 2)].reshape(32, D) for f in first], axis=0)
+        values = jnp.dot(swap[...], values, preferred_element_type=F32)
         parts = project(values, norm_t, wt, qg_t, kg_t)
-        at = pl.ds(pl.multiple_of(xs * 8, 8), 8)
+        at = pl.ds(pl.multiple_of(d * 8, 8), 8)
         for ref, part in zip((tq, tk, tv), parts):
             ref[:, at, :] = part.astype(F32).reshape(16, 8, INNER)
         return carry
@@ -225,14 +242,11 @@
     lax.fori_loop(0, 4, time_attend, 0)
 
     def time_mix(j, carry):
-        zls = [rem(x + j + 4 - a, 4) for a in range(4)]
-        first = [a * 8 + zls[a] * 2 for a in range(4)]
-        parts = []
-        for a in range(4):
-            rows = lax.broadcasted_iota(jnp.int32, (32, 512), 0)
-            cols = lax.broadcasted_iota(jnp.int32, (32, 512), 1)
-            parts.append(cols == (rows & 15) * 32 + (rows >> 4) + first[a])
-        pick = jnp.concatenate([jnp.where(part, 1.0, 0.0).astype(BF) for part in parts], axis=0)
+        d = rem(x + j, 4)
+        first = pairs_of(d)
+        rows = lax.broadcasted_iota(jnp.int32, (128, 512), 0)
+        cols = lax.broadcasted_iota(jnp.int32, (128, 512), 1)
+        pick = jnp.where(cols == (rows & 15) * 32 + (rows >> 4) + d * 8, 1.0, 0.0).astype(BF)
         attended = jnp.dot(pick, tatt[...], preferred_element_type=F32).astype(BF)
         delta = jnp.dot(attended, wo[...], preferred_element_type=F32)
         for a in range(4):
@@ -356,33 +370,11 @@
 
     lax.fori_loop(0, 4, space_attend, 0)
 
-    def finish(i, carry):
-        wait_local(home.at[2 * i], home.at[2 * i], r4.at[2 * i])
-        wait_local(home.at[2 * i + 1], home.at[2 * i + 1], r4.at[2 * i + 1])
-        for half in range(2):
-            for n in range(2):
-                at = (3 * half + n) * 128
-                out[i, 0, :, at : at + 128] = home[2 * i + half, 8 * n : 8 * n + 8].reshape(128, 128)
-        low = home[2 * i, 16:].reshape(64, 128).astype(F32)
-        high = home[2 * i + 1, 16:].reshape(64, 128).astype(F32)
-        left = lane[:, :128] < 64
-        out[i, 0, :64, 256:384] = jnp.where(left, low, high).astype(BF)
-        out[i, 0, 64:, 256:384] = pltpu.roll(jnp.where(left, high, low), 64, 1).astype(BF)
-        return carry
-
-    lax.fori_loop(0, 4, finish, 0)
-
-    def done1(i, carry):
-        device, src = copy1(i)
-
-        @pl.when(not_me(device))
-        def _():
-            pltpu.make_async_remote_copy(
-                src_ref=src, dst_ref=tok.at[frame], send_sem=s1.at[i], recv_sem=r1.at[frame],
-                device_id=device, device_id_type=MESH,
-            ).wait_send()
-
-        return carry
+    def arrived(i, carry):
+        wait_local(home.at[i], home.at[i], r4.at[i])
+        return carry
+
+    lax.fori_loop(0, 8, arrived, 0)
 
     def done2(f, carry):
         device = target2(f)
@@ -412,10 +404,22 @@
 
         return carry
 
-    lax.fori_loop(0, 32, done1, 0)
+    lax.fori_loop(16, 32, sent1, 0)
     lax.fori_loop(0, 32, done2, 0)
     lax.fori_loop(0, 4, done3, 0)
     lax.fori_loop(0, 8, done4, 0)
+
+
+def assemble(home, out):
+    for half in range(2):
+        for n in range(2):
+            at = (3 * half + n) * 128
+            out[0, 0, :, at : at + 128] = home[half, 8 * n : 8 * n + 8].reshape(128, 128)
+    low = home[0, 16:].reshape(64, 128).astype(F32)
+    high = home[1, 16:].reshape(64, 128).astype(F32)
+    left = lax.broadcasted_iota(jnp.int32, (1, 128), 1) < 64
+    out[0, 0, :64, 256:384] = jnp.where(left, low, high).astype(BF)
+    out[0, 0, 64:, 256:384] = pltpu.roll(jnp.where(left, high, low), 64, 1).astype(BF)
 
 
 def body(
@@ -425,12 +429,11 @@
     anywhere = pl.BlockSpec(memory_space=pl.ANY)
     vmem = pl.BlockSpec(memory_space=pltpu.VMEM)
     dma = pltpu.SemaphoreType.DMA
-    flat = lambda gain: gain.reshape(1, -1)
-    return pl.pallas_call(
+    home = pl.pallas_call(
         kernel,
-        out_shape=jax.ShapeDtypeStruct((4, 1, 128, INNER), BF),
+        out_shape=jax.ShapeDtypeStruct((8, 20, 16, 128), BF),
         in_specs=[anywhere, vmem, anywhere, vmem, vmem, anywhere, vmem, anywhere, vmem, vmem],
-        out_specs=vmem,
+        out_specs=anywhere,
         scratch_shapes=[
             pltpu.VMEM((D, 3 * INNER), BF),
             pltpu.VMEM((INNER, D), BF),
@@ -449,7 +452,6 @@
             pltpu.VMEM((2, 4, 3, 8, 16, HALF), BF),
             pltpu.VMEM((4, 1024, 256), BF),
             pltpu.VMEM((8, 20, 16, 128), BF),
-            pltpu.VMEM((8, 20, 16, 128), BF),
             dma((3,)),
             dma((32,)), dma((32,)),
             dma((32,)), dma((32,)),
@@ -463,9 +465,16 @@
             flops=2 * 512 * D * (6 * INNER + INNER), bytes_accessed=14 * 2**20, transcendentals=6 * 2**20
         ),
     )(
-        clip, flat(norm_time), w_time_qkv, flat(q_gain_time), flat(k_gain_time), w_time_out,
-        flat(norm_space), w_space_qkv, flat(q_gain_space), flat(k_gain_space),
+        clip, norm_time, w_time_qkv, q_gain_time, k_gain_time, w_time_out,
+        norm_space, w_space_qkv, q_gain_space, k_gain_space,
     )
+    return pl.pallas_call(
+        assemble,
+        grid=(4,),
+        out_shape=jax.ShapeDtypeStruct((4, 1, 128, INNER), BF),
+        in_specs=[pl.BlockSpec((2, 20, 16, 128), lambda i: (i, 0, 0, 0))],
+        out_specs=pl.BlockSpec((1, 1, 128, INNER), lambda i: (i, 0, 0, 0)),
+    )(home)
 
 
 def solution(mesh):

time: 112 us -> 96.3 us (0.86)
  local copies, waits for them, and re-layouts: 9.61 us -> 0 us
  Pallas kernels: 100 us -> 94.9 us
    reshape x6 -> x0, local copies, waits for them, and re-layouts: 7.63 us -> none  [body(): flat = lambda gain: gain.reshape(1, -1)]
    pallas_call x1 -> x2, Pallas kernels: 100 us -> 94.9 us  [the longest x1 91.5 us: body(): pl.pallas_call(kernel, out_shape=jax.ShapeDtypeStruct((8, 20, 16, 128), B...]
    unnamed x1 -> x0, local copies, waits for them, and re-layouts: 1.98 us -> none
where the time goes in v3:
time: 96.3 us; the launch traced here: 94.9 us
  Pallas kernels  94.9 us (99%)
    pallas_call x1, Pallas kernels, body(): pl.pallas_call(kernel, out_shape=jax.ShapeDtypeStruct((8, 20, 16, 128), B...  91.5 us
    pallas_call x1, Pallas kernels, body(): pl.pallas_call(assemble, grid=(4,), out_shape=jax.ShapeDtypeStruct((4, 1,...  3.34 us

profile of v3, /device:TPU:1, one launch (start us, length us, event | category | flops | bytes accessed | tf_op | source)
XLA Modules:
  0.0 94.9 jit_solution(12989186251461731073)
XLA Ops:
  0.0 91.5 %shard_map.100.home = bf16[8,20,16,128]{3,2,1,0:T(8,128)(2,1)} custom-call(bf16[4,1,128,1280]{3,2,1,0:T(8,128)(2,1)} %clip.1, f32[1280]{0:T(1024)} %norm_t.1, bf16[1280,1920]{1,0:T(8,128)(2,1)} %w_tqkv.1, f32[640]{0:T(1024)} %qg_t.1, f32[640]{0:T(1024)} %kg_t.1, bf16[640,1280]{1,0:T(8,128)(2,1)} %w_out.1, f32[1280]{0:T(1024)} %norm_s.1, ...), custom_call_target="tpu_custom_call" | custom-call | flops 5872025600 | bytes 14680064 | tf_op jit(solution)/shard_map/pallas_call | solution.py:432
  91.5 3.3 %shard_map.101 = bf16[4,1,128,640]{3,2,1,0:T(8,128)(2,1)} custom-call(bf16[8,20,16,128]{3,2,1,0:T(8,128)(2,1)} %shard_map.100.home), custom_call_target="tpu_custom_call" | custom-call | tf_op jit(solution)/shard_map/pallas_call | solution.py:471

commit v4 on v3

v4 whole, which is shorter than its diff:
```python
import math

import jax
import jax.numpy as jnp
from jax import lax
from jax.experimental import pallas as pl
from jax.experimental.pallas import tpu as pltpu
from jax.sharding import PartitionSpec as P

MESH = pl.DeviceIdType.MESH
HDIM = 80
HEADS = 8
D = 1280
INNER = 640
HALF = 384
EPS = 1e-06
SCALE = HDIM ** (-0.5) * math.log2(math.e)
BF = jnp.bfloat16
F32 = jnp.float32
WINDOWS = (0, 0, 128, 128, 256, 256, 384, 384)


def div(a, b):
    return lax.div(a, jnp.int32(b))


def rem(a, b):
    return lax.rem(a, jnp.int32(b))


def kernel(
    clip, norm_t, w_tqkv, qg_t, kg_t, w_out, norm_s, w_sqkv, qg_s, kg_s,
    home,
    wt, wo, ws, blocks, pmask, swap, tok, tq, tkv, tatt, mixed, tok2, send_qkv, qkv, vm, att,
    wsem, s1, r1, st, rt, s2, r2, sq, rq, s4, r4,
):
    frame, patch = lax.axis_index("frame"), lax.axis_index("patch")
    x, zl, core = div(frame, 8), rem(div(frame, 2), 4), rem(frame, 2)
    zh, y = div(patch, 4), rem(patch, 4)
    z = zh * 4 + zl
    c, zb = div(z, 2), rem(z, 2)

    def flip(zz, cc):
        return rem(zz + 1 + rem(div(cc + 1, 2), 2), 2)

    zh_src = flip(zb, c)
    pg_src = zh_src * 4 + y

    def is_me(device):
        return (device[0] == frame) & (device[1] == patch)

    def not_me(device):
        return (device[0] != frame) | (device[1] != patch)

    def target1(i):
        xt = rem(x + zl + 4 - div(rem(i, 16), 4), 4)
        ct = rem(c + 1 + i, 4)
        zt = 2 * ct + flip(zh, ct)
        device = (xt * 8 + rem(zt, 4) * 2 + core, div(zt, 4) * 4 + y)
        return device, ct, div(i, 16) * 4 + xt

    def source1(i):
        return (i * 2 + core, pg_src)

    def target2(m):
        zt = 2 * c + core
        yt = rem(rem(m, 4) + c + 2 * core, 4)
        return (div(m, 4) * 8 + rem(zt, 4) * 2 + rem(x, 2), div(zt, 4) * 4 + yt)

    def source2(i):
        xs, zs = 2 * div(i, 8) + core, 2 * c + rem(i, 2)
        return (xs * 8 + rem(zs, 4) * 2 + zb, div(zs, 4) * 4 + rem(div(i, 2), 4))

    home_zl = rem(y + 8 - c - 2 * zb, 4)
    home_frame = x * 8 + home_zl * 2 + zb

    def target4(g):
        return (home_frame, g)

    def source4(i):
        zs = 2 * div(i, 2) + core
        return (x * 8 + rem(zs, 4) * 2 + rem(i, 2), div(zs, 4) * 4 + rem(zl + div(i, 2) + 2 * core, 4))

    partner = (x * 8 + zl * 2 + 1 - core, patch)

    loads = (
        pltpu.make_async_copy(w_tqkv, wt, wsem.at[0]),
        pltpu.make_async_copy(w_out, wo, wsem.at[1]),
        pltpu.make_async_copy(w_sqkv, ws, wsem.at[2]),
    )
    loads[0].start()
    loads[1].start()
    loads[2].start()

    barrier = pltpu.get_barrier_semaphore()

    def greet(device):
        @pl.when(not_me(device))
        def _():
            pl.semaphore_signal(barrier, inc=1, device_id=device, device_id_type=MESH)

    def greet1(i, carry):
        greet(source1(i))
        return carry

    def greet2(i, carry):
        greet(source2(i))
        return carry

    def greet4(i, carry):
        greet(source4(i))
        return carry

    lax.fori_loop(0, 16, greet1, 0)
    lax.fori_loop(0, 16, greet2, 0)
    lax.fori_loop(0, 8, greet4, 0)
    greet(partner)

    rows = lax.broadcasted_iota(jnp.int32, (INNER, INNER), 0)
    cols = lax.broadcasted_iota(jnp.int32, (INNER, INNER), 1)
    head_of = lambda v: lax.shift_right_logical(v * 52429, 22)
    blocks[...] = jnp.where(head_of(rows) == head_of(cols), 1.0, 0.0).astype(BF)
    rows = lax.broadcasted_iota(jnp.int32, (128, 256), 0)
    cols = lax.broadcasted_iota(jnp.int32, (128, 256), 1)
    pmask[...] = jnp.where((rows >> 4) == ((cols & 127) >> 4), 1.0, 0.0).astype(BF)
    rows = lax.broadcasted_iota(jnp.int32, (256, 256), 0)
    cols = lax.broadcasted_iota(jnp.int32, (256, 256), 1)
    swap[...] = jnp.where(cols == (rows & 15) * 16 + (rows >> 4), 1.0, 0.0).astype(BF)

    own1 = jnp.where(zh_src == zh, 1, 0)
    own4 = jnp.where(home_frame == frame, 1, 0)
    own2 = jnp.where((core == zb) & (core == rem(x, 2)), 1, 0)
    pl.semaphore_wait(barrier, 16 - own1 + 16 - own2 + 8 - own4 + 1)

    def copy1(i):
        device, ct, b = target1(i)
        src = clip.at[ct, 0, pl.ds(pl.multiple_of(b * 16, 16), 16)]
        return device, src

    def send1(i, carry):
        device, src = copy1(i)
        slot = div(i, 16) * 16 + div(frame, 2)

        @pl.when(not_me(device))
        def _():
            pltpu.make_async_remote_copy(
                src_ref=src, dst_ref=tok.at[slot], send_sem=s1.at[i], recv_sem=r1.at[slot],
                device_id=device, device_id_type=MESH,
            ).start()

        @pl.when(is_me(device))
        def _():
            pltpu.make_async_copy(src, tok.at[slot], r1.at[slot]).start()

        return carry

    def sent1(i, carry):
        device, src = copy1(i)

        @pl.when(not_me(device))
        def _():
            pltpu.make_async_remote_copy(
                src_ref=src, dst_ref=tok.at[0], send_sem=s1.at[i], recv_sem=r1.at[0],
                device_id=device, device_id_type=MESH,
            ).wait_send()

        return carry

    lax.fori_loop(0, 16, send1, 0)

    def layer_norm(values, gain):
        average = jnp.mean(values, axis=-1, keepdims=True)
        centred = values - average
        variance = jnp.mean(centred * centred, axis=-1, keepdims=True)
        return (centred * lax.rsqrt(variance + EPS) * gain).astype(BF)

    def head_norm(part, gain):
        squares = jnp.dot((part * part).astype(BF), blocks[...], preferred_element_type=F32)
        return (part * lax.rsqrt(squares * (1.0 / HDIM) + EPS) * gain).astype(BF)

    def queries(normed, weight, gain):
        product = jnp.dot(normed, weight[:, :INNER], preferred_element_type=F32)
        return head_norm(product, gain[...].reshape(1, -1))

    def keys_values(normed, weight, gain):
        product = jnp.dot(normed, weight[:, INNER:], preferred_element_type=F32)
        return head_norm(product[:, :INNER], gain[...].reshape(1, -1)), product[:, INNER:].astype(BF)

    def wait_local(src, dst, sem):
        pltpu.make_async_copy(src, dst, sem).wait()

    for load in loads:
        load.wait()

    lane = lax.broadcasted_iota(jnp.int32, (1, 256), 1)

    def exchange_time(batch):
        return pltpu.make_async_remote_copy(
            src_ref=tkv.at[batch, core], dst_ref=tkv.at[batch, core], send_sem=st.at[batch],
            recv_sem=rt.at[batch], device_id=partner, device_id_type=MESH,
        )

    def time_attend(batch, g):
        rows = pl.ds(pl.multiple_of(g * 128, 128), 128)
        tiles = [jnp.zeros((128, 128), F32)] * 5
        for h in range(HEADS):
            w = WINDOWS[h]
            first = h * HDIM - w
            mask = (lane >= first) & (lane < first + HDIM)
            spare = 255 if first + HDIM <= 255 else 0
            query = jnp.where(mask, tq[rows, w : w + 256], 0.0).astype(BF)
            keys = tkv[batch, :, 0, rows, w : w + 256].reshape(256, 256)
            scores = lax.dot_general(
                query, keys, (((1,), (1,)), ((), ())), preferred_element_type=F32
            )
            prob = jnp.exp2(scores * SCALE).astype(BF) * pmask[...]
            vals = tkv[batch, :, 1, rows, w : w + 256].reshape(256, 256)
            vals = jnp.where(mask, vals, 1.0).astype(BF)
            summed = jnp.dot(prob, vals, preferred_element_type=F32)
            result = summed * (1.0 / summed[:, spare : spare + 1])
            t = w // 128
            tiles[t] = jnp.where(mask[:, :128], result[:, :128], tiles[t])
            tiles[t + 1] = jnp.where(mask[:, 128:], result[:, 128:], tiles[t + 1])
        for n in range(5):
            tatt[rows, n * 128 : (n + 1) * 128] = tiles[n].astype(BF)

    def send2(batch, m):
        f = batch * 16 + m
        device = target2(m)
        slot = batch * 16 + div(x, 2) * 8 + pg_src

        @pl.when(not_me(device))
        def _():
            pltpu.make_async_remote_copy(
                src_ref=mixed.at[f], dst_ref=tok2.at[slot], send_sem=s2.at[f],
                recv_sem=r2.at[slot], device_id=device, device_id_type=MESH,
            ).start()

        @pl.when(is_me(device))
        def _():
            pltpu.make_async_copy(mixed.at[f], tok2.at[slot], r2.at[slot]).start()

    def time_step(batch, carry):
        @pl.when(batch == 0)
        def _():
            for j in range(2):
                lax.fori_loop(8 * j, 8 * j + 8, sent1, 0)
                lax.fori_loop(8 * j + 16, 8 * j + 24, send1, 0)

        def wait(i, inner):
            slot = batch * 16 + i
            wait_local(tok.at[slot], tok.at[slot], r1.at[slot])
            return inner

        lax.fori_loop(0, 16, wait, 0)
        values = tok[pl.ds(batch * 16, 16)].reshape(256, D)
        values = jnp.dot(swap[...], values, preferred_element_type=F32)
        normed = layer_norm(values, norm_t[...].reshape(1, -1))
        for n, part in enumerate(keys_values(normed, wt, kg_t)):
            tkv[batch, core, n] = part
        exchange_time(batch).start()
        tq[...] = queries(normed, wt, qg_t)
        wait_local(tkv.at[batch, core], tkv.at[batch, 1 - core], rt.at[batch])

        def attend(g, inner):
            time_attend(batch, g)
            return inner

        lax.fori_loop(0, 2, attend, 0)

        def mix(half, inner):
            rows = pl.ds(pl.multiple_of(half * 128, 128), 128)
            attended = jnp.dot(swap[rows, :], tatt[...], preferred_element_type=F32).astype(BF)
            delta = jnp.dot(attended, wo[...], preferred_element_type=F32)
            at = pl.ds(batch * 16 + half * 8, 8)
            total = (tok[at].reshape(128, D).astype(F32) + delta).astype(BF)
            mixed[at] = total.reshape(8, 16, D)

            def send(i, deeper):
                send2(batch, half * 8 + rem(i, 2) * 4 + rem(div(i, 2) + x + y, 4))
                return deeper

            lax.fori_loop(0, 8, send, 0)
            return inner

        lax.fori_loop(0, 2, mix, 0)
        return carry

    lax.fori_loop(0, 2, time_step, 0)

    def exchange(batch, part):
        at = pl.ds(batch * 2, 2)
        which = pl.ds(0, 1) if part == 0 else pl.ds(1, 2)
        return pltpu.make_async_remote_copy(
            src_ref=send_qkv.at[at, which], dst_ref=qkv.at[core, at, which],
            send_sem=sq.at[batch, part], recv_sem=rq.at[batch, part],
            device_id=partner, device_id_type=MESH,
        )

    def space_step(batch, carry):
        def wait(i, inner):
            slot = batch * 16 + i
            wait_local(tok2.at[slot], tok2.at[slot], r2.at[slot])
            return inner

        lax.fori_loop(0, 16, wait, 0)
        values = tok2[pl.ds(batch * 16, 16)].reshape(256, D).astype(F32)
        normed = layer_norm(values, norm_s[...].reshape(1, -1))

        def keep(n, part):
            low, high = part[:, :HALF], part[:, INNER - HALF :]
            mine = jnp.where(core == 0, low, high).reshape(2, 8, 16, HALF)
            other = jnp.where(core == 0, high, low).reshape(2, 8, 16, HALF)
            for i in range(2):
                qkv[core, batch * 2 + i, n] = mine[i]
                send_qkv[batch * 2 + i, n] = other[i]

        for n, part in enumerate(keys_values(normed, ws, kg_s)):
            keep(1 + n, part)
        exchange(batch, 1).start()
        keep(0, queries(normed, ws, qg_s))
        exchange(batch, 0).start()
        return carry

    lax.fori_loop(0, 2, space_step, 0)

    def wait_partner(batch, carry):
        at = pl.ds(batch * 2, 2)
        for part, which in enumerate((pl.ds(0, 1), pl.ds(1, 2))):
            wait_local(send_qkv.at[at, which], qkv.at[1 - core, at, which], rq.at[batch, part])
        return carry

    lax.fori_loop(0, 2, wait_partner, 0)

    def head_mask(j):
        first = j * HDIM + 64 * core - (0 if j < 2 else 128)
        return (lane >= first) & (lane < first + HDIM)

    for j in range(4):
        w = 0 if j < 2 else 128
        vals = qkv[:, :, 2, :, :, w : w + 256].reshape(1024, 256)
        vm[j] = jnp.where(head_mask(j), vals, 1.0).astype(BF)

    def send4(g):
        device = target4(g)
        slot = c * 2 + core
        src, dst = att.at[g], home.at[slot]

        @pl.when(not_me(device))
        def _():
            pltpu.make_async_remote_copy(
                src_ref=src, dst_ref=dst, send_sem=s4.at[g], recv_sem=r4.at[slot],
                device_id=device, device_id_type=MESH,
            ).start()

        @pl.when(is_me(device))
        def _():
            pltpu.make_async_copy(src, dst, r4.at[slot]).start()

    def space_attend(j, carry):
        t = rem(zl + j, 4)
        tiles = [jnp.zeros((256, 128), F32)] * 3
        for h in range(4):
            w = 0 if h < 2 else 128
            spare = 255 if h < 2 else 0
            mask = head_mask(h)
            query = qkv[:, :, 0, pl.ds(2 * t, 2), :, w : w + 256].reshape(256, 256)
            query = jnp.where(mask, query, 0.0).astype(BF)
            keys = qkv[:, :, 1, :, :, w : w + 256].reshape(1024, 256)
            scores = lax.dot_general(
                query, keys, (((1,), (1,)), ((), ())), preferred_element_type=F32
            )
            prob = jnp.exp2(scores * SCALE).astype(BF)
            summed = jnp.dot(prob, vm[h], preferred_element_type=F32)
            result = summed * (1.0 / summed[:, spare : spare + 1])
            n = w // 128
            tiles[n] = jnp.where(mask[:, :128], result[:, :128], tiles[n])
            tiles[n + 1] = jnp.where(mask[:, 128:], result[:, 128:], tiles[n + 1])
        first = core == 0
        whole = [jnp.where(first, tiles[n], tiles[n + 1]).astype(BF) for n in range(2)]
        shared = jnp.where(first, tiles[2], tiles[0])
        packed = shared[:128] + pltpu.roll(shared[128:], 64, 1)
        packed = packed.astype(BF).reshape(4, 2, 16, 128)
        for g in range(2):
            for n in range(2):
                att[2 * t + g, 8 * n : 8 * n + 8] = whole[n].reshape(8, 2, 16, 128)[:, g]
            att[2 * t + g, 16:] = packed[:, g]
        send4(2 * t)
        send4(2 * t + 1)
        return carry

    lax.fori_loop(0, 4, space_attend, 0)

    def arrived(i, carry):
        wait_local(home.at[i], home.at[i], r4.at[i])
        return carry

    lax.fori_loop(0, 8, arrived, 0)

    def done2(f, carry):
        device = target2(rem(f, 16))

        @pl.when(not_me(device))
        def _():
            pltpu.make_async_remote_copy(
                src_ref=mixed.at[f], dst_ref=tok2.at[f], send_sem=s2.at[f], recv_sem=r2.at[f],
                device_id=device, device_id_type=MESH,
            ).wait_send()

        return carry

    def done3(batch, carry):
        exchange_time(batch).wait_send()
        exchange(batch, 0).wait_send()
        exchange(batch, 1).wait_send()
        return carry

    def done4(g, carry):
        device = target4(g)

        @pl.when(not_me(device))
        def _():
            pltpu.make_async_remote_copy(
                src_ref=att.at[g], dst_ref=home.at[0], send_sem=s4.at[g], recv_sem=r4.at[0],
                device_id=device, device_id_type=MESH,
            ).wait_send()

        return carry

    lax.fori_loop(16, 32, sent1, 0)
    lax.fori_loop(0, 32, done2, 0)
    lax.fori_loop(0, 2, done3, 0)
    lax.fori_loop(0, 8, done4, 0)


def assemble(home, out):
    def place(blocks, core, at):
        for n in range(4):
            row = (n // 2 * 4 + n % 2 * 2 + core) * 16
            out[i, 0, row : row + 16, at : at + 128] = blocks[n]

    left = lax.broadcasted_iota(jnp.int32, (1, 128), 1) < 64
    for i in range(4):
        for core in range(2):
            for half in range(2):
                for n in range(2):
                    place(home[2 * i + half, 8 * n + 4 * core : 8 * n + 4 * core + 4], core, (3 * half + n) * 128)
        low = home[2 * i, 16:].reshape(64, 128).astype(F32)
        high = home[2 * i + 1, 16:].reshape(64, 128).astype(F32)
        place(jnp.where(left, low, high).astype(BF).reshape(4, 16, 128), 0, 256)
        rolled = pltpu.roll(jnp.where(left, high, low), 64, 1)
        place(rolled.astype(BF).reshape(4, 16, 128), 1, 256)


def body(
    clip, norm_time, w_time_qkv, q_gain_time, k_gain_time, w_time_out,
    norm_space, w_space_qkv, q_gain_space, k_gain_space,
):
    anywhere = pl.BlockSpec(memory_space=pl.ANY)
    vmem = pl.BlockSpec(memory_space=pltpu.VMEM)
    dma = pltpu.SemaphoreType.DMA
    home = pl.pallas_call(
        kernel,
        out_shape=jax.ShapeDtypeStruct((8, 20, 16, 128), BF),
        in_specs=[anywhere, vmem, anywhere, vmem, vmem, anywhere, vmem, anywhere, vmem, vmem],
        out_specs=anywhere,
        scratch_shapes=[
            pltpu.VMEM((D, 3 * INNER), BF),
            pltpu.VMEM((INNER, D), BF),
            pltpu.VMEM((D, 3 * INNER), BF),
            pltpu.VMEM((INNER, INNER), BF),
            pltpu.VMEM((128, 256), BF),
            pltpu.VMEM((256, 256), BF),
            pltpu.VMEM((32, 16, D), BF),
            pltpu.VMEM((256, INNER), BF),
            pltpu.VMEM((2, 2, 2, 256, INNER), BF),
            pltpu.VMEM((256, INNER), BF),
            pltpu.VMEM((32, 16, D), BF),
            pltpu.VMEM((32, 16, D), BF),
            pltpu.VMEM((4, 3, 8, 16, HALF), BF),
            pltpu.VMEM((2, 4, 3, 8, 16, HALF), BF),
            pltpu.VMEM((4, 1024, 256), BF),
            pltpu.VMEM((8, 20, 16, 128), BF),
            dma((3,)),
            dma((32,)), dma((32,)),
            dma((2,)), dma((2,)),
            dma((32,)), dma((32,)),
            dma((2, 2)), dma((2, 2)),
            dma((8,)), dma((8,)),
        ],
        compiler_params=pltpu.CompilerParams(
            collective_id=0, has_side_effects=True, vmem_limit_bytes=58 * 2**20
        ),
        cost_estimate=pl.CostEstimate(
            flops=2 * 512 * D * (6 * INNER + INNER), bytes_accessed=14 * 2**20, transcendentals=6 * 2**20
        ),
    )(
        clip, norm_time, w_time_qkv, q_gain_time, k_gain_time, w_time_out,
        norm_space, w_space_qkv, q_gain_space, k_gain_space,
    )
    return pl.pallas_call(
        assemble,
        out_shape=jax.ShapeDtypeStruct((4, 1, 128, INNER), BF),
        in_specs=[vmem],
        out_specs=vmem,
    )(home)


def solution(mesh):
    in_specs = (P(None, "frame", "patch", None),) + (P(),) * 9
    out_specs = P(None, "frame", "patch", None)
    return jax.shard_map(body, mesh=mesh, in_specs=in_specs, out_specs=out_specs, check_vma=False)
```

time: 96.3 us -> 92.9 us (0.965)
  the two profiles are of different devices: /device:TPU:1 before, /device:TPU:94 now
where the time goes in v4:
time: 92.9 us; the launch traced here: 92.8 us
  Pallas kernels  92.8 us (100%)
    pallas_call x1, Pallas kernels, body(): pl.pallas_call(kernel, out_shape=jax.ShapeDtypeStruct((8, 20, 16, 128), B...  90.7 us
    pallas_call x1, Pallas kernels, body(): pl.pallas_call(assemble, out_shape=jax.ShapeDtypeStruct((4, 1, 128, INNER...  2.04 us

profile of v4, /device:TPU:94, one launch (start us, length us, event | category | flops | bytes accessed | tf_op | source)
XLA Modules:
  0.0 92.8 jit_solution(9703757211808953096)
XLA Ops:
  0.0 90.7 %shard_map.100.home = bf16[8,20,16,128]{3,2,1,0:T(8,128)(2,1)} custom-call(bf16[4,1,128,1280]{3,2,1,0:T(8,128)(2,1)} %clip.1, f32[1280]{0:T(1024)} %norm_t.1, bf16[1280,1920]{1,0:T(8,128)(2,1)} %w_tqkv.1, f32[640]{0:T(1024)} %qg_t.1, f32[640]{0:T(1024)} %kg_t.1, bf16[640,1280]{1,0:T(8,128)(2,1)} %w_out.1, f32[1280]{0:T(1024)} %norm_s.1, ...), custom_call_target="tpu_custom_call" | custom-call | flops 5872025600 | bytes 14680064 | tf_op jit(solution)/shard_map/pallas_call | solution.py:462
  90.7 2.0 %shard_map.101 = bf16[4,1,128,640]{3,2,1,0:T(8,128)(2,1)} custom-call(bf16[8,20,16,128]{3,2,1,0:T(8,128)(2,1)} %shard_map.100.home), custom_call_target="tpu_custom_call" | custom-call | tf_op jit(solution)/shard_map/pallas_call | solution.py:501

commit v5 on v4

--- a/solution.py
+++ b/solution.py
@@ -67,6 +67,10 @@
         yt = rem(rem(m, 4) + c + 2 * core, 4)
         return (div(m, 4) * 8 + rem(zt, 4) * 2 + rem(x, 2), div(zt, 4) * 4 + yt)
 
+    def order2(i):
+        xt = rem(x + 1 + 2 * div(i, 8) + rem(i, 2), 4)
+        return xt * 4 + rem(div(i, 2) + x + y, 4)
+
     def source2(i):
         xs, zs = 2 * div(i, 8) + core, 2 * c + rem(i, 2)
         return (xs * 8 + rem(zs, 4) * 2 + zb, div(zs, 4) * 4 + rem(div(i, 2), 4))
@@ -122,10 +126,10 @@
     blocks[...] = jnp.where(head_of(rows) == head_of(cols), 1.0, 0.0).astype(BF)
     rows = lax.broadcasted_iota(jnp.int32, (128, 256), 0)
     cols = lax.broadcasted_iota(jnp.int32, (128, 256), 1)
-    pmask[...] = jnp.where((rows >> 4) == ((cols & 127) >> 4), 1.0, 0.0).astype(BF)
-    rows = lax.broadcasted_iota(jnp.int32, (256, 256), 0)
-    cols = lax.broadcasted_iota(jnp.int32, (256, 256), 1)
-    swap[...] = jnp.where(cols == (rows & 15) * 16 + (rows >> 4), 1.0, 0.0).astype(BF)
+    pmask[...] = jnp.where(((rows >> 3) & 7) == ((cols >> 3) & 7), 1.0, 0.0).astype(BF)
+    rows = lax.broadcasted_iota(jnp.int32, (128, 128), 0)
+    cols = lax.broadcasted_iota(jnp.int32, (128, 128), 1)
+    swap[...] = jnp.where(cols == (rows & 7) * 16 + (rows >> 3), 1.0, 0.0).astype(BF)
 
     own1 = jnp.where(zh_src == zh, 1, 0)
     own4 = jnp.where(home_frame == frame, 1, 0)
@@ -194,27 +198,28 @@
 
     lane = lax.broadcasted_iota(jnp.int32, (1, 256), 1)
 
-    def exchange_time(batch):
+    def exchange_time(batch, j):
         return pltpu.make_async_remote_copy(
-            src_ref=tkv.at[batch, core], dst_ref=tkv.at[batch, core], send_sem=st.at[batch],
-            recv_sem=rt.at[batch], device_id=partner, device_id_type=MESH,
+            src_ref=tkv.at[batch, core, :, j], dst_ref=tkv.at[batch, core, :, j],
+            send_sem=st.at[batch, j], recv_sem=rt.at[batch, j],
+            device_id=partner, device_id_type=MESH,
         )
 
     def time_attend(batch, g):
-        rows = pl.ds(pl.multiple_of(g * 128, 128), 128)
+        rows = pl.ds(pl.multiple_of(g * 64, 64), 64)
         tiles = [jnp.zeros((128, 128), F32)] * 5
         for h in range(HEADS):
             w = WINDOWS[h]
             first = h * HDIM - w
             mask = (lane >= first) & (lane < first + HDIM)
             spare = 255 if first + HDIM <= 255 else 0
-            query = jnp.where(mask, tq[rows, w : w + 256], 0.0).astype(BF)
-            keys = tkv[batch, :, 0, rows, w : w + 256].reshape(256, 256)
+            query = jnp.where(mask, tq[:, rows, w : w + 256].reshape(128, 256), 0.0).astype(BF)
+            keys = tkv[batch, :, 0, :, rows, w : w + 256].reshape(256, 256)
             scores = lax.dot_general(
                 query, keys, (((1,), (1,)), ((), ())), preferred_element_type=F32
             )
             prob = jnp.exp2(scores * SCALE).astype(BF) * pmask[...]
-            vals = tkv[batch, :, 1, rows, w : w + 256].reshape(256, 256)
+            vals = tkv[batch, :, 1, :, rows, w : w + 256].reshape(256, 256)
             vals = jnp.where(mask, vals, 1.0).astype(BF)
             summed = jnp.dot(prob, vals, preferred_element_type=F32)
             result = summed * (1.0 / summed[:, spare : spare + 1])
@@ -222,7 +227,7 @@
             tiles[t] = jnp.where(mask[:, :128], result[:, :128], tiles[t])
             tiles[t + 1] = jnp.where(mask[:, 128:], result[:, 128:], tiles[t + 1])
         for n in range(5):
-            tatt[rows, n * 128 : (n + 1) * 128] = tiles[n].astype(BF)
+            tatt[:, rows, n * 128 : (n + 1) * 128] = tiles[n].astype(BF).reshape(2, 64, 128)
 
     def send2(batch, m):
         f = batch * 16 + m
@@ -247,20 +252,24 @@
                 lax.fori_loop(8 * j, 8 * j + 8, sent1, 0)
                 lax.fori_loop(8 * j + 16, 8 * j + 24, send1, 0)
 
-        def wait(i, inner):
-            slot = batch * 16 + i
-            wait_local(tok.at[slot], tok.at[slot], r1.at[slot])
+        def project(j, inner):
+            slots = [
+                batch * 16 + a * 4 + rem(x + 2 * j + k + 4 - a, 4) for a in range(4) for k in range(2)
+            ]
+            for slot in slots:
+                wait_local(tok.at[slot], tok.at[slot], r1.at[slot])
+            values = jnp.concatenate([tok[slot] for slot in slots], axis=0)
+            values = jnp.dot(swap[...], values, preferred_element_type=F32)
+            normed = layer_norm(values, norm_t[...].reshape(1, -1))
+            for n, part in enumerate(keys_values(normed, wt, kg_t)):
+                tkv[batch, core, n, j] = part
+            exchange_time(batch, j).start()
+            tq[j] = queries(normed, wt, qg_t)
             return inner
 
-        lax.fori_loop(0, 16, wait, 0)
-        values = tok[pl.ds(batch * 16, 16)].reshape(256, D)
-        values = jnp.dot(swap[...], values, preferred_element_type=F32)
-        normed = layer_norm(values, norm_t[...].reshape(1, -1))
-        for n, part in enumerate(keys_values(normed, wt, kg_t)):
-            tkv[batch, core, n] = part
-        exchange_time(batch).start()
-        tq[...] = queries(normed, wt, qg_t)
-        wait_local(tkv.at[batch, core], tkv.at[batch, 1 - core], rt.at[batch])
+        lax.fori_loop(0, 2, project, 0)
+        for j in range(2):
+            wait_local(tkv.at[batch, core, :, j], tkv.at[batch, 1 - core, :, j], rt.at[batch, j])
 
         def attend(g, inner):
             time_attend(batch, g)
@@ -269,15 +278,23 @@
         lax.fori_loop(0, 2, attend, 0)
 
         def mix(half, inner):
-            rows = pl.ds(pl.multiple_of(half * 128, 128), 128)
-            attended = jnp.dot(swap[rows, :], tatt[...], preferred_element_type=F32).astype(BF)
+            near = [rem(x + 1 + 2 * half + i, 4) for i in range(2)]
+            rows = lax.broadcasted_iota(jnp.int32, (128, 256), 0)
+            cols = lax.broadcasted_iota(jnp.int32, (128, 256), 1)
+            a = jnp.where(rows < 64, near[0], near[1])
+            d = (a + (rows >> 4) + 8 - x) & 3
+            source = (d >> 1) * 128 + (rows & 15) * 8 + a * 2 + (d & 1)
+            pick = jnp.where(cols == source, 1.0, 0.0).astype(BF)
+            attended = tatt[...].reshape(256, INNER)
+            attended = jnp.dot(pick, attended, preferred_element_type=F32).astype(BF)
             delta = jnp.dot(attended, wo[...], preferred_element_type=F32)
-            at = pl.ds(batch * 16 + half * 8, 8)
-            total = (tok[at].reshape(128, D).astype(F32) + delta).astype(BF)
-            mixed[at] = total.reshape(8, 16, D)
+            for i in range(2):
+                at = pl.ds(batch * 16 + near[i] * 4, 4)
+                total = (tok[at].reshape(64, D).astype(F32) + delta[64 * i : 64 * i + 64]).astype(BF)
+                mixed[at] = total.reshape(4, 16, D)
 
             def send(i, deeper):
-                send2(batch, half * 8 + rem(i, 2) * 4 + rem(div(i, 2) + x + y, 4))
+                send2(batch, order2(half * 8 + i))
                 return deeper
 
             lax.fori_loop(0, 8, send, 0)
@@ -288,49 +305,48 @@
 
     lax.fori_loop(0, 2, time_step, 0)
 
-    def exchange(batch, part):
-        at = pl.ds(batch * 2, 2)
+    def exchange(n, part):
         which = pl.ds(0, 1) if part == 0 else pl.ds(1, 2)
         return pltpu.make_async_remote_copy(
-            src_ref=send_qkv.at[at, which], dst_ref=qkv.at[core, at, which],
-            send_sem=sq.at[batch, part], recv_sem=rq.at[batch, part],
+            src_ref=send_qkv.at[n, which], dst_ref=qkv.at[core, n, which],
+            send_sem=sq.at[n, part], recv_sem=rq.at[n, part],
             device_id=partner, device_id_type=MESH,
         )
 
-    def space_step(batch, carry):
+    def space_step(j, carry):
+        early = rem(x + 3 - rem(x + core + 1, 2), 4)
+        quarter = div(j, 2) * 2 + rem(div(early, 2) + j, 2)
+
         def wait(i, inner):
-            slot = batch * 16 + i
+            slot = quarter * 8 + i
             wait_local(tok2.at[slot], tok2.at[slot], r2.at[slot])
             return inner
 
-        lax.fori_loop(0, 16, wait, 0)
-        values = tok2[pl.ds(batch * 16, 16)].reshape(256, D).astype(F32)
+        lax.fori_loop(0, 8, wait, 0)
+        values = tok2[pl.ds(quarter * 8, 8)].reshape(128, D).astype(F32)
         normed = layer_norm(values, norm_s[...].reshape(1, -1))
 
         def keep(n, part):
             low, high = part[:, :HALF], part[:, INNER - HALF :]
-            mine = jnp.where(core == 0, low, high).reshape(2, 8, 16, HALF)
-            other = jnp.where(core == 0, high, low).reshape(2, 8, 16, HALF)
-            for i in range(2):
-                qkv[core, batch * 2 + i, n] = mine[i]
-                send_qkv[batch * 2 + i, n] = other[i]
+            mine, other = jnp.where(core == 0, low, high), jnp.where(core == 0, high, low)
+            qkv[core, quarter, n] = mine.reshape(2, 4, 16, HALF)
+            send_qkv[quarter, n] = other.reshape(2, 4, 16, HALF)
 
         for n, part in enumerate(keys_values(normed, ws, kg_s)):
             keep(1 + n, part)
-        exchange(batch, 1).start()
+        exchange(quarter, 1).start()
         keep(0, queries(normed, ws, qg_s))
-        exchange(batch, 0).start()
-        return carry
-
-    lax.fori_loop(0, 2, space_step, 0)
-
-    def wait_partner(batch, carry):
-        at = pl.ds(batch * 2, 2)
+        exchange(quarter, 0).start()
+        return carry
+
+    lax.fori_loop(0, 4, space_step, 0)
+
+    def wait_partner(n, carry):
         for part, which in enumerate((pl.ds(0, 1), pl.ds(1, 2))):
-            wait_local(send_qkv.at[at, which], qkv.at[1 - core, at, which], rq.at[batch, part])
-        return carry
-
-    lax.fori_loop(0, 2, wait_partner, 0)
+            wait_local(send_qkv.at[n, which], qkv.at[1 - core, n, which], rq.at[n, part])
+        return carry
+
+    lax.fori_loop(0, 4, wait_partner, 0)
 
     def head_mask(j):
         first = j * HDIM + 64 * core - (0 if j < 2 else 128)
@@ -338,7 +354,7 @@
 
     for j in range(4):
         w = 0 if j < 2 else 128
-        vals = qkv[:, :, 2, :, :, w : w + 256].reshape(1024, 256)
+        vals = qkv[:, :, 2, :, :, :, w : w + 256].reshape(1024, 256)
         vm[j] = jnp.where(head_mask(j), vals, 1.0).astype(BF)
 
     def send4(g):
@@ -358,15 +374,15 @@
             pltpu.make_async_copy(src, dst, r4.at[slot]).start()
 
     def space_attend(j, carry):
-        t = rem(zl + j, 4)
+        t = rem(y + z + j, 4)
         tiles = [jnp.zeros((256, 128), F32)] * 3
         for h in range(4):
             w = 0 if h < 2 else 128
             spare = 255 if h < 2 else 0
             mask = head_mask(h)
-            query = qkv[:, :, 0, pl.ds(2 * t, 2), :, w : w + 256].reshape(256, 256)
+            query = qkv[:, :, 0, :, t, :, w : w + 256].reshape(256, 256)
             query = jnp.where(mask, query, 0.0).astype(BF)
-            keys = qkv[:, :, 1, :, :, w : w + 256].reshape(1024, 256)
+            keys = qkv[:, :, 1, :, :, :, w : w + 256].reshape(1024, 256)
             scores = lax.dot_general(
                 query, keys, (((1,), (1,)), ((), ())), preferred_element_type=F32
             )
@@ -383,10 +399,10 @@
         packed = packed.astype(BF).reshape(4, 2, 16, 128)
         for g in range(2):
             for n in range(2):
-                att[2 * t + g, 8 * n : 8 * n + 8] = whole[n].reshape(8, 2, 16, 128)[:, g]
-            att[2 * t + g, 16:] = packed[:, g]
-        send4(2 * t)
-        send4(2 * t + 1)
+                att[4 * g + t, 8 * n : 8 * n + 8] = whole[n].reshape(8, 2, 16, 128)[:, g]
+            att[4 * g + t, 16:] = packed[:, g]
+        send4(t)
+        send4(4 + t)
         return carry
 
     lax.fori_loop(0, 4, space_attend, 0)
@@ -409,10 +425,10 @@
 
         return carry
 
-    def done3(batch, carry):
-        exchange_time(batch).wait_send()
-        exchange(batch, 0).wait_send()
-        exchange(batch, 1).wait_send()
+    def done3(n, carry):
+        exchange_time(div(n, 2), rem(n, 2)).wait_send()
+        exchange(n, 0).wait_send()
+        exchange(n, 1).wait_send()
         return carry
 
     def done4(g, carry):
@@ -429,18 +445,26 @@
 
     lax.fori_loop(16, 32, sent1, 0)
     lax.fori_loop(0, 32, done2, 0)
-    lax.fori_loop(0, 2, done3, 0)
+    lax.fori_loop(0, 4, done3, 0)
     lax.fori_loop(0, 8, done4, 0)
 
 
-def assemble(home, out):
+def assemble(home_hbm, out_hbm, home, out, arrive, leave):
     def place(blocks, core, at):
         for n in range(4):
             row = (n // 2 * 4 + n % 2 * 2 + core) * 16
             out[i, 0, row : row + 16, at : at + 128] = blocks[n]
 
     left = lax.broadcasted_iota(jnp.int32, (1, 128), 1) < 64
+    copies = [
+        pltpu.make_async_copy(home_hbm.at[pl.ds(2 * i, 2)], home.at[pl.ds(2 * i, 2)], arrive.at[i])
+        for i in range(4)
+    ]
+    results = [pltpu.make_async_copy(out.at[i], out_hbm.at[i], leave.at[i]) for i in range(4)]
+    for copy in copies:
+        copy.start()
     for i in range(4):
+        copies[i].wait()
         for core in range(2):
             for half in range(2):
                 for n in range(2):
@@ -450,6 +474,9 @@
         place(jnp.where(left, low, high).astype(BF).reshape(4, 16, 128), 0, 256)
         rolled = pltpu.roll(jnp.where(left, high, low), 64, 1)
         place(rolled.astype(BF).reshape(4, 16, 128), 1, 256)
+        results[i].start()
+    for result in results:
+        result.wait()
 
 
 def body(
@@ -470,22 +497,22 @@
             pltpu.VMEM((D, 3 * INNER), BF),
             pltpu.VMEM((INNER, INNER), BF),
             pltpu.VMEM((128, 256), BF),
-            pltpu.VMEM((256, 256), BF),
+            pltpu.VMEM((128, 128), BF),
             pltpu.VMEM((32, 16, D), BF),
-            pltpu.VMEM((256, INNER), BF),
-            pltpu.VMEM((2, 2, 2, 256, INNER), BF),
-            pltpu.VMEM((256, INNER), BF),
+            pltpu.VMEM((2, 128, INNER), BF),
+            pltpu.VMEM((2, 2, 2, 2, 128, INNER), BF),
+            pltpu.VMEM((2, 128, INNER), BF),
             pltpu.VMEM((32, 16, D), BF),
             pltpu.VMEM((32, 16, D), BF),
-            pltpu.VMEM((4, 3, 8, 16, HALF), BF),
-            pltpu.VMEM((2, 4, 3, 8, 16, HALF), BF),
+            pltpu.VMEM((4, 3, 2, 4, 16, HALF), BF),
+            pltpu.VMEM((2, 4, 3, 2, 4, 16, HALF), BF),
             pltpu.VMEM((4, 1024, 256), BF),
             pltpu.VMEM((8, 20, 16, 128), BF),
             dma((3,)),
             dma((32,)), dma((32,)),
-            dma((2,)), dma((2,)),
+            dma((2, 2)), dma((2, 2)),
             dma((32,)), dma((32,)),
-            dma((2, 2)), dma((2, 2)),
+            dma((4, 2)), dma((4, 2)),
             dma((8,)), dma((8,)),
         ],
         compiler_params=pltpu.CompilerParams(
@@ -501,8 +528,13 @@
     return pl.pallas_call(
         assemble,
         out_shape=jax.ShapeDtypeStruct((4, 1, 128, INNER), BF),
-        in_specs=[vmem],
-        out_specs=vmem,
+        in_specs=[anywhere],
+        out_specs=anywhere,
+        scratch_shapes=[
+            pltpu.VMEM((8, 20, 16, 128), BF),
+            pltpu.VMEM((4, 1, 128, INNER), BF),
+            dma((4,)), dma((4,)),
+        ],
     )(home)
 
 

time: 92.9 us -> 90.7 us (0.976)
  the two profiles are of different devices: /device:TPU:94 before, /device:TPU:1 now
where the time goes in v5:
time: 90.7 us; the launch traced here: 90.6 us
  Pallas kernels  90.6 us (100%)
    pallas_call x1, Pallas kernels, body(): pl.pallas_call(kernel, out_shape=jax.ShapeDtypeStruct((8, 20, 16, 128), B...  88.6 us
    pallas_call x1, Pallas kernels, body(): pl.pallas_call(assemble, out_shape=jax.ShapeDtypeStruct((4, 1, 128, INNER...  1.97 us

profile of v5, /device:TPU:1, one launch (start us, length us, event | category | flops | bytes accessed | tf_op | source)
XLA Modules:
  0.0 90.6 jit_solution(3185051341931579716)
XLA Ops:
  0.0 88.6 %shard_map.100.home_hbm = bf16[8,20,16,128]{3,2,1,0:T(8,128)(2,1)} custom-call(bf16[4,1,128,1280]{3,2,1,0:T(8,128)(2,1)} %clip.1, f32[1280]{0:T(1024)} %norm_t.1, bf16[1280,1920]{1,0:T(8,128)(2,1)} %w_tqkv.1, f32[640]{0:T(1024)} %qg_t.1, f32[640]{0:T(1024)} %kg_t.1, bf16[640,1280]{1,0:T(8,128)(2,1)} %w_out.1, f32[1280]{0:T(1024)} %norm_s.1, ...), custom_call_target="tpu_custom_call" | custom-call | flops 5872025600 | bytes 14680064 | tf_op jit(solution)/shard_map/pallas_call | solution.py:489
  88.6 2.0 %shard_map.101 = bf16[4,1,128,640]{3,2,1,0:T(8,128)(2,1)} custom-call(bf16[8,20,16,128]{3,2,1,0:T(8,128)(2,1)} %shard_map.100.home_hbm), custom_call_target="tpu_custom_call" | custom-call | tf_op jit(solution)/shard_map/pallas_call | solution.py:528

commit v6 on v5

--- a/solution.py
+++ b/solution.py
@@ -120,6 +120,47 @@
     lax.fori_loop(0, 8, greet4, 0)
     greet(partner)
 
+    own1 = jnp.where(zh_src == zh, 1, 0)
+    own4 = jnp.where(home_frame == frame, 1, 0)
+    own2 = jnp.where((core == zb) & (core == rem(x, 2)), 1, 0)
+    pl.semaphore_wait(barrier, 16 - own1 + 16 - own2 + 8 - own4 + 1)
+
+    def copy1(i):
+        device, ct, b = target1(i)
+        src = clip.at[ct, 0, pl.ds(pl.multiple_of(b * 16, 16), 16)]
+        return device, src
+
+    def send1(i, carry):
+        device, src = copy1(i)
+        slot = div(i, 16) * 16 + div(frame, 2)
+
+        @pl.when(not_me(device))
+        def _():
+            pltpu.make_async_remote_copy(
+                src_ref=src, dst_ref=tok.at[slot], send_sem=s1.at[i], recv_sem=r1.at[slot],
+                device_id=device, device_id_type=MESH,
+            ).start()
+
+        @pl.when(is_me(device))
+        def _():
+            pltpu.make_async_copy(src, tok.at[slot], r1.at[slot]).start()
+
+        return carry
+
+    def sent1(i, carry):
+        device, src = copy1(i)
+
+        @pl.when(not_me(device))
+        def _():
+            pltpu.make_async_remote_copy(
+                src_ref=src, dst_ref=tok.at[0], send_sem=s1.at[i], recv_sem=r1.at[0],
+                device_id=device, device_id_type=MESH,
+            ).wait_send()
+
+        return carry
+
+    lax.fori_loop(0, 16, send1, 0)
+
     rows = lax.broadcasted_iota(jnp.int32, (INNER, INNER), 0)
     cols = lax.broadcasted_iota(jnp.int32, (INNER, INNER), 1)
     head_of = lambda v: lax.shift_right_logical(v * 52429, 22)
@@ -130,47 +171,6 @@
     rows = lax.broadcasted_iota(jnp.int32, (128, 128), 0)
     cols = lax.broadcasted_iota(jnp.int32, (128, 128), 1)
     swap[...] = jnp.where(cols == (rows & 7) * 16 + (rows >> 3), 1.0, 0.0).astype(BF)
-
-    own1 = jnp.where(zh_src == zh, 1, 0)
-    own4 = jnp.where(home_frame == frame, 1, 0)
-    own2 = jnp.where((core == zb) & (core == rem(x, 2)), 1, 0)
-    pl.semaphore_wait(barrier, 16 - own1 + 16 - own2 + 8 - own4 + 1)
-
-    def copy1(i):
-        device, ct, b = target1(i)
-        src = clip.at[ct, 0, pl.ds(pl.multiple_of(b * 16, 16), 16)]
-        return device, src
-
-    def send1(i, carry):
-        device, src = copy1(i)
-        slot = div(i, 16) * 16 + div(frame, 2)
-
-        @pl.when(not_me(device))
-        def _():
-            pltpu.make_async_remote_copy(
-                src_ref=src, dst_ref=tok.at[slot], send_sem=s1.at[i], recv_sem=r1.at[slot],
-                device_id=device, device_id_type=MESH,
-            ).start()
-
-        @pl.when(is_me(device))
-        def _():
-            pltpu.make_async_copy(src, tok.at[slot], r1.at[slot]).start()
-
-        return carry
-
-    def sent1(i, carry):
-        device, src = copy1(i)
-
-        @pl.when(not_me(device))
-        def _():
-            pltpu.make_async_remote_copy(
-                src_ref=src, dst_ref=tok.at[0], send_sem=s1.at[i], recv_sem=r1.at[0],
-                device_id=device, device_id_type=MESH,
-            ).wait_send()
-
-        return carry
-
-    lax.fori_loop(0, 16, send1, 0)
 
     def layer_norm(values, gain):
         average = jnp.mean(values, axis=-1, keepdims=True)
@@ -374,7 +374,7 @@
             pltpu.make_async_copy(src, dst, r4.at[slot]).start()
 
     def space_attend(j, carry):
-        t = rem(y + z + j, 4)
+        t = rem(y + 1 + j, 4)
         tiles = [jnp.zeros((256, 128), F32)] * 3
         for h in range(4):
             w = 0 if h < 2 else 128
@@ -401,17 +401,11 @@
             for n in range(2):
                 att[4 * g + t, 8 * n : 8 * n + 8] = whole[n].reshape(8, 2, 16, 128)[:, g]
             att[4 * g + t, 16:] = packed[:, g]
-        send4(t)
-        send4(4 + t)
+        send4((1 - zh) * 4 + t)
+        send4(zh * 4 + t)
         return carry
 
     lax.fori_loop(0, 4, space_attend, 0)
-
-    def arrived(i, carry):
-        wait_local(home.at[i], home.at[i], r4.at[i])
-        return carry
-
-    lax.fori_loop(0, 8, arrived, 0)
 
     def done2(f, carry):
         device = target2(rem(f, 16))
@@ -447,6 +441,12 @@
     lax.fori_loop(0, 32, done2, 0)
     lax.fori_loop(0, 4, done3, 0)
     lax.fori_loop(0, 8, done4, 0)
+
+    def arrived(i, carry):
+        wait_local(home.at[i], home.at[i], r4.at[i])
+        return carry
+
+    lax.fori_loop(0, 8, arrived, 0)
 
 
 def assemble(home_hbm, out_hbm, home, out, arrive, leave):

time: 90.7 us -> 90 us (level)
  no operation moved by 1% of the time
where the time goes in v6:
time: 90 us; the launch traced here: 89.9 us
  Pallas kernels  89.9 us (100%)
    pallas_call x1, Pallas kernels, body(): pl.pallas_call(kernel, out_shape=jax.ShapeDtypeStruct((8, 20, 16, 128), B...  87.9 us
    pallas_call x1, Pallas kernels, body(): pl.pallas_call(assemble, out_shape=jax.ShapeDtypeStruct((4, 1, 128, INNER...  1.97 us

profile of v6, /device:TPU:1, one launch (start us, length us, event | category | flops | bytes accessed | tf_op | source)
XLA Modules:
  0.0 89.9 jit_solution(13470250902722374644)
XLA Ops:
  0.0 87.9 %shard_map.100.home_hbm = bf16[8,20,16,128]{3,2,1,0:T(8,128)(2,1)} custom-call(bf16[4,1,128,1280]{3,2,1,0:T(8,128)(2,1)} %clip.1, f32[1280]{0:T(1024)} %norm_t.1, bf16[1280,1920]{1,0:T(8,128)(2,1)} %w_tqkv.1, f32[640]{0:T(1024)} %qg_t.1, f32[640]{0:T(1024)} %kg_t.1, bf16[640,1280]{1,0:T(8,128)(2,1)} %w_out.1, f32[1280]{0:T(1024)} %norm_s.1, ...), custom_call_target="tpu_custom_call" | custom-call | flops 5872025600 | bytes 14680064 | tf_op jit(solution)/shard_map/pallas_call | solution.py:489
  87.9 2.0 %shard_map.101 = bf16[4,1,128,640]{3,2,1,0:T(8,128)(2,1)} custom-call(bf16[8,20,16,128]{3,2,1,0:T(8,128)(2,1)} %shard_map.100.home_hbm), custom_call_target="tpu_custom_call" | custom-call | tf_op jit(solution)/shard_map/pallas_call | solution.py:528

commit v7 on v6

--- a/solution.py
+++ b/solution.py
@@ -159,7 +159,7 @@
 
         return carry
 
-    lax.fori_loop(0, 16, send1, 0)
+    lax.fori_loop(0, 16, send1, 0, unroll=True)
 
     rows = lax.broadcasted_iota(jnp.int32, (INNER, INNER), 0)
     cols = lax.broadcasted_iota(jnp.int32, (INNER, INNER), 1)
@@ -275,7 +275,7 @@
             time_attend(batch, g)
             return inner
 
-        lax.fori_loop(0, 2, attend, 0)
+        lax.fori_loop(0, 2, attend, 0, unroll=True)
 
         def mix(half, inner):
             near = [rem(x + 1 + 2 * half + i, 4) for i in range(2)]
@@ -297,10 +297,10 @@
                 send2(batch, order2(half * 8 + i))
                 return deeper
 
-            lax.fori_loop(0, 8, send, 0)
+            lax.fori_loop(0, 8, send, 0, unroll=True)
             return inner
 
-        lax.fori_loop(0, 2, mix, 0)
+        lax.fori_loop(0, 2, mix, 0, unroll=True)
         return carry
 
     lax.fori_loop(0, 2, time_step, 0)
@@ -322,7 +322,7 @@
             wait_local(tok2.at[slot], tok2.at[slot], r2.at[slot])
             return inner
 
-        lax.fori_loop(0, 8, wait, 0)
+        lax.fori_loop(0, 8, wait, 0, unroll=True)
         values = tok2[pl.ds(quarter * 8, 8)].reshape(128, D).astype(F32)
         normed = layer_norm(values, norm_s[...].reshape(1, -1))
 

time: 90 us -> 87.7 us (0.974)
  Pallas kernels: 89.9 us -> 87.2 us
    pallas_call x1, Pallas kernels: 87.9 us -> 85.2 us  [body(): pl.pallas_call(kernel, out_shape=jax.ShapeDtypeStruct((8, 20, 16, 128), B...]
where the time goes in v7:
time: 87.7 us; the launch traced here: 87.2 us
  Pallas kernels  87.2 us (99%)
    pallas_call x1, Pallas kernels, body(): pl.pallas_call(kernel, out_shape=jax.ShapeDtypeStruct((8, 20, 16, 128), B...  85.2 us
    pallas_call x1, Pallas kernels, body(): pl.pallas_call(assemble, out_shape=jax.ShapeDtypeStruct((4, 1, 128, INNER...  1.97 us

profile of v7, /device:TPU:1, one launch (start us, length us, event | category | flops | bytes accessed | tf_op | source)
XLA Modules:
  0.0 87.2 jit_solution(9335229070234048883)
XLA Ops:
  0.0 85.2 %shard_map.100.home_hbm = bf16[8,20,16,128]{3,2,1,0:T(8,128)(2,1)} custom-call(bf16[4,1,128,1280]{3,2,1,0:T(8,128)(2,1)} %clip.1, f32[1280]{0:T(1024)} %norm_t.1, bf16[1280,1920]{1,0:T(8,128)(2,1)} %w_tqkv.1, f32[640]{0:T(1024)} %qg_t.1, f32[640]{0:T(1024)} %kg_t.1, bf16[640,1280]{1,0:T(8,128)(2,1)} %w_out.1, f32[1280]{0:T(1024)} %norm_s.1, ...), custom_call_target="tpu_custom_call" | custom-call | flops 5872025600 | bytes 14680064 | tf_op jit(solution)/shard_map/pallas_call | solution.py:489
  85.2 2.0 %shard_map.101 = bf16[4,1,128,640]{3,2,1,0:T(8,128)(2,1)} custom-call(bf16[8,20,16,128]{3,2,1,0:T(8,128)(2,1)} %shard_map.100.home_hbm), custom_call_target="tpu_custom_call" | custom-call | tf_op jit(solution)/shard_map/pallas_call | solution.py:528

commit v8 on v7

--- a/solution.py
+++ b/solution.py
@@ -115,9 +115,9 @@
         greet(source4(i))
         return carry
 
-    lax.fori_loop(0, 16, greet1, 0)
-    lax.fori_loop(0, 16, greet2, 0)
-    lax.fori_loop(0, 8, greet4, 0)
+    lax.fori_loop(0, 16, greet1, 0, unroll=True)
+    lax.fori_loop(0, 16, greet2, 0, unroll=True)
+    lax.fori_loop(0, 8, greet4, 0, unroll=True)
     greet(partner)
 
     own1 = jnp.where(zh_src == zh, 1, 0)
@@ -249,8 +249,8 @@
         @pl.when(batch == 0)
         def _():
             for j in range(2):
-                lax.fori_loop(8 * j, 8 * j + 8, sent1, 0)
-                lax.fori_loop(8 * j + 16, 8 * j + 24, send1, 0)
+                lax.fori_loop(8 * j, 8 * j + 8, sent1, 0, unroll=True)
+                lax.fori_loop(8 * j + 16, 8 * j + 24, send1, 0, unroll=True)
 
         def project(j, inner):
             slots = [

time: 87.7 us -> 87.2 us (level)
  no operation moved by 1% of the time
where the time goes in v8:
time: 87.2 us; the launch traced here: 86.4 us
  Pallas kernels  86.4 us (99%)
    pallas_call x1, Pallas kernels, body(): pl.pallas_call(kernel, out_shape=jax.ShapeDtypeStruct((8, 20, 16, 128), B...  84.4 us
    pallas_call x1, Pallas kernels, body(): pl.pallas_call(assemble, out_shape=jax.ShapeDtypeStruct((4, 1, 128, INNER...  1.97 us

profile of v8, /device:TPU:1, one launch (start us, length us, event | category | flops | bytes accessed | tf_op | source)
XLA Modules:
  0.0 86.4 jit_solution(6306051355724108383)
XLA Ops:
  0.0 84.4 %shard_map.100.home_hbm = bf16[8,20,16,128]{3,2,1,0:T(8,128)(2,1)} custom-call(bf16[4,1,128,1280]{3,2,1,0:T(8,128)(2,1)} %clip.1, f32[1280]{0:T(1024)} %norm_t.1, bf16[1280,1920]{1,0:T(8,128)(2,1)} %w_tqkv.1, f32[640]{0:T(1024)} %qg_t.1, f32[640]{0:T(1024)} %kg_t.1, bf16[640,1280]{1,0:T(8,128)(2,1)} %w_out.1, f32[1280]{0:T(1024)} %norm_s.1, ...), custom_call_target="tpu_custom_call" | custom-call | flops 5872025600 | bytes 14680064 | tf_op jit(solution)/shard_map/pallas_call | solution.py:489
  84.4 2.0 %shard_map.101 = bf16[4,1,128,640]{3,2,1,0:T(8,128)(2,1)} custom-call(bf16[8,20,16,128]{3,2,1,0:T(8,128)(2,1)} %shard_map.100.home_hbm), custom_call_target="tpu_custom_call" | custom-call | tf_op jit(solution)/shard_map/pallas_call | solution.py:528

commit v9 on v8

--- a/solution.py
+++ b/solution.py
@@ -346,7 +346,7 @@
             wait_local(send_qkv.at[n, which], qkv.at[1 - core, n, which], rq.at[n, part])
         return carry
 
-    lax.fori_loop(0, 4, wait_partner, 0)
+    lax.fori_loop(0, 4, wait_partner, 0, unroll=True)
 
     def head_mask(j):
         first = j * HDIM + 64 * core - (0 if j < 2 else 128)
@@ -446,7 +446,7 @@
         wait_local(home.at[i], home.at[i], r4.at[i])
         return carry
 
-    lax.fori_loop(0, 8, arrived, 0)
+    lax.fori_loop(0, 8, arrived, 0, unroll=True)
 
 
 def assemble(home_hbm, out_hbm, home, out, arrive, leave):

time: 87.2 us -> 87.3 us (level)
  no operation moved by 1% of the time
where the time goes in v9:
time: 87.3 us; the launch traced here: 86.3 us
  Pallas kernels  86.3 us (99%)
    pallas_call x1, Pallas kernels, body(): pl.pallas_call(kernel, out_shape=jax.ShapeDtypeStruct((8, 20, 16, 128), B...  84.4 us
    pallas_call x1, Pallas kernels, body(): pl.pallas_call(assemble, out_shape=jax.ShapeDtypeStruct((4, 1, 128, INNER...  1.97 us

profile of v9, /device:TPU:1, one launch (start us, length us, event | category | flops | bytes accessed | tf_op | source)
XLA Modules:
  0.0 86.3 jit_solution(5147693992866062854)
XLA Ops:
  0.0 84.4 %shard_map.100.home_hbm = bf16[8,20,16,128]{3,2,1,0:T(8,128)(2,1)} custom-call(bf16[4,1,128,1280]{3,2,1,0:T(8,128)(2,1)} %clip.1, f32[1280]{0:T(1024)} %norm_t.1, bf16[1280,1920]{1,0:T(8,128)(2,1)} %w_tqkv.1, f32[640]{0:T(1024)} %qg_t.1, f32[640]{0:T(1024)} %kg_t.1, bf16[640,1280]{1,0:T(8,128)(2,1)} %w_out.1, f32[1280]{0:T(1024)} %norm_s.1, ...), custom_call_target="tpu_custom_call" | custom-call | flops 5872025600 | bytes 14680064 | tf_op jit(solution)/shard_map/pallas_call | solution.py:489
  84.4 2.0 %shard_map.101 = bf16[4,1,128,640]{3,2,1,0:T(8,128)(2,1)} custom-call(bf16[8,20,16,128]{3,2,1,0:T(8,128)(2,1)} %shard_map.100.home_hbm), custom_call_target="tpu_custom_call" | custom-call | tf_op jit(solution)/shard_map/pallas_call | solution.py:528
